TPU v7x, 32 devices: a whole 2x2x4 slice. The times are simulated.
32 devices in a mesh: dp: 2 (over x), seq: 16 (over z, y, core).
Axes of the slice: x: 2, y: 2, z: 4, core: 2. Of those that a mesh axis runs over, the one named last changes fastest.
Arguments:
- spatial_qkv: bfloat16 [3, 4096, 1536], P(None, ('dp', 'seq')), parts along dimension 1, may hold values from -6 to 6
- temporal_qkv: bfloat16 [3, 4096, 1536], P(None, ('dp', 'seq')), parts along dimension 1, may hold values from -6 to 6
- cross_query: bfloat16 [4096, 1536], P(('dp', 'seq')), parts along dimension 0, may hold values from -6 to 6
- caption_kv: bfloat16 [640, 2, 1536], P(('dp', 'seq')), parts along dimension 0, may hold values from -6 to 6
- out_grad: bfloat16 [4096, 1536], P(('dp', 'seq')), parts along dimension 0, may hold values from -6 to 6
- live_tokens: int32 [2], P('dp'), parts along dimension 0, may hold values from 512 to 2048, as said below
- caption_len: int32 [2], P('dp'), parts along dimension 0, may hold values from 80 to 320, as said below
Outputs:
- mixed: bfloat16 [4096, 1536], P(('dp', 'seq')), parts along dimension 0
- spatial_grads: bfloat16 [3, 4096, 1536], P(None, ('dp', 'seq')), parts along dimension 1
- temporal_grads: bfloat16 [3, 4096, 1536], P(None, ('dp', 'seq')), parts along dimension 1
- cross_query_grad: bfloat16 [4096, 1536], P(('dp', 'seq')), parts along dimension 0
- caption_grads: float32 [640, 2, 1536], P(('dp', 'seq')), parts along dimension 0
There are 2 independent parts, one for each index of `dp`. A program takes and returns all parts, laid end to end along the dimension named above; each array names one. Nothing has to cross between parts.
Inputs may be any that keep to these rules, and one draw needn't show every extreme that they name: Tokens from live_tokens on are padding. Caption rows from caption_len on are padding.
All inputs are finite; a program needn't handle non-finite values.
Results may differ from a plain program's by a relative error of at most 0.035.
Values may be sent and summed in bfloat16 or wider, within the bound.
A program may use at most 128 MiB of HBM per device.

v0:
```python
import jax
import jax.numpy as jnp
from jax import lax
from jax.sharding import PartitionSpec as P

HDIM = 128
P_SIZE = 512


def swapped(shard, axis, apart):
    return lax.ppermute(shard, axis, [(i, i ^ 1 << apart) for i in range(lax.axis_size(axis))])


def score_rows(queries, key_rows, key_keep):
    scale_factor = queries.shape[-1] ** (-0.5)
    scores = (
        jnp.einsum("bnhe,bmhe->bhnm", queries, key_rows, preferred_element_type=jnp.float32)
        * scale_factor
    )
    return jnp.where(key_keep, scores, -1e30)


def weight_rows(scores, largest, denominator):
    weights = jnp.exp(scores - largest[..., None]) / denominator[..., None]
    return (weights, weights.astype(jnp.bfloat16))


def slope_rows(weights, grad_rows, value_rows, row_delta):
    dprobs = jnp.einsum(
        "bnhe,bmhe->bhnm", grad_rows, value_rows, preferred_element_type=jnp.float32
    )
    return (weights * (dprobs - row_delta[..., None])).astype(jnp.bfloat16)


def attend_forward(queries, key_rows, value_rows, grad_rows, key_keep):
    scale_factor = queries.shape[-1] ** (-0.5)
    scores = score_rows(queries, key_rows, key_keep)
    largest = jnp.max(scores, axis=-1)
    denominator = jnp.sum(jnp.exp(scores - largest[..., None]), axis=-1)
    weights, weights_low = weight_rows(scores, largest, denominator)
    branch = jnp.einsum(
        "bhnm,bmhe->bnhe", weights_low, value_rows, preferred_element_type=jnp.float32
    ).astype(jnp.bfloat16)
    row_delta = jnp.einsum("bnhe,bnhe->bhn", grad_rows, branch, preferred_element_type=jnp.float32)
    dscores = slope_rows(weights, grad_rows, value_rows, row_delta)
    query_grad = (
        jnp.einsum("bhnm,bmhe->bnhe", dscores, key_rows, preferred_element_type=jnp.float32)
        * scale_factor
    )
    return (branch, query_grad, weights_low, dscores, largest, denominator, row_delta)


def key_terms(queries, grad_rows, weights_low, dscores):
    scale_factor = queries.shape[-1] ** (-0.5)
    key_grad = (
        jnp.einsum("bhnm,bnhe->bmhe", dscores, queries, preferred_element_type=jnp.float32)
        * scale_factor
    )
    value_grad = jnp.einsum(
        "bhnm,bnhe->bmhe", weights_low, grad_rows, preferred_element_type=jnp.float32
    )
    return (key_grad, value_grad)


def ordered(low_half, mine, theirs, axis_number):
    return jnp.where(
        low_half,
        jnp.concatenate([mine, theirs], axis=axis_number),
        jnp.concatenate([theirs, mine], axis=axis_number),
    )


def local(spatial_qkv, temporal_qkv, cross_query, caption_kv, out_grad, live_tokens, caption_len):
    devices = lax.axis_size("seq")
    dev_index = lax.axis_index("seq")
    tok_rows = out_grad.shape[0]
    feature_width = out_grad.shape[1]
    head_count = feature_width // HDIM
    token_ids = dev_index * tok_rows + jnp.arange(tok_rows)
    live_rows = token_ids < live_tokens[0]
    grad_rows = jnp.where(live_rows[:, None], out_grad, jnp.zeros_like(out_grad))

    def split_heads(tensor, batch_count):
        return tensor.reshape(batch_count, -1, head_count, HDIM)

    def join_heads(tensor):
        return tensor.reshape(tok_rows, feature_width)

    group_bits = (P_SIZE // tok_rows).bit_length() - 1
    every_key = jnp.ones((P_SIZE,), jnp.bool_)
    frame_kv = spatial_qkv[1:3]
    for bit_number in range(group_bits):
        partner = swapped(frame_kv, "seq", bit_number)
        low_half = dev_index // 2**bit_number % 2 == 0
        frame_kv = ordered(low_half, frame_kv, partner, 1)
    own_queries = split_heads(spatial_qkv[0], 1)
    own_grad = split_heads(grad_rows, 1)
    results = attend_forward(
        own_queries, split_heads(frame_kv[0], 1), split_heads(frame_kv[1], 1), own_grad, every_key
    )
    spatial_out, spatial_dq = (results[0], results[1])
    key_part, value_part = key_terms(own_queries, own_grad, results[2], results[3])
    grad_sums = jnp.stack(
        [key_part.reshape(P_SIZE, feature_width), value_part.reshape(P_SIZE, feature_width)]
    )
    for bit_number in reversed(range(group_bits)):
        half_rows = grad_sums.shape[1] // 2
        up_half = dev_index // 2**bit_number % 2
        kept_half = lax.dynamic_slice_in_dim(grad_sums, up_half * half_rows, half_rows, 1)
        sent_half = lax.dynamic_slice_in_dim(grad_sums, (1 - up_half) * half_rows, half_rows, 1)
        grad_sums = kept_half + swapped(sent_half.astype(jnp.bfloat16), "seq", bit_number).astype(
            sent_half.dtype
        )
    key_grad, value_grad = (grad_sums[0], grad_sums[1])
    spatial_grads = jnp.stack(
        [join_heads(spatial_dq), join_heads(key_grad), join_heads(value_grad)]
    ).astype(jnp.bfloat16)
    piece_rows = tok_rows // devices

    def pixel_split(tensor):
        return tensor.reshape(piece_rows, devices, head_count, HDIM)

    parts = (
        lax.all_to_all(
            pixel_split(temporal_qkv[0]), "seq", split_axis=1, concat_axis=0, tiled=True
        ),
        lax.all_to_all(
            pixel_split(temporal_qkv[1]), "seq", split_axis=1, concat_axis=0, tiled=True
        ),
        lax.all_to_all(
            pixel_split(temporal_qkv[2]), "seq", split_axis=1, concat_axis=0, tiled=True
        ),
        lax.all_to_all(pixel_split(grad_rows), "seq", split_axis=1, concat_axis=0, tiled=True),
    )
    pixels_here = P_SIZE // devices
    frame_total = tok_rows // pixels_here
    item_heads = parts[0].shape[2]

    def by_pixel(tensor):
        return jnp.swapaxes(tensor.reshape(frame_total, pixels_here, item_heads, HDIM), 0, 1)

    def back_rows(tensor):
        return jnp.swapaxes(tensor, 0, 1).reshape(tok_rows, 1, item_heads, HDIM)

    pixel_here_ids = jnp.arange(pixels_here) * devices + dev_index
    frame_keep = (
        jnp.arange(frame_total)[None, :] * P_SIZE + pixel_here_ids[:, None] < live_tokens[0]
    )
    frame_keep = frame_keep.reshape(pixels_here, 1, 1, frame_total)
    pixel_queries = by_pixel(parts[0])
    pixel_grad = by_pixel(parts[3])
    outcome = attend_forward(
        pixel_queries, by_pixel(parts[1]), by_pixel(parts[2]), pixel_grad, frame_keep
    )
    pixel_kgrad, pixel_vgrad = key_terms(pixel_queries, pixel_grad, outcome[2], outcome[3])
    temporal_grads = jnp.stack(
        [
            join_heads(
                lax.all_to_all(
                    back_rows(outcome[1]).astype(jnp.bfloat16),
                    "seq",
                    split_axis=0,
                    concat_axis=1,
                    tiled=True,
                )
            ),
            join_heads(
                lax.all_to_all(
                    back_rows(pixel_kgrad).astype(jnp.bfloat16),
                    "seq",
                    split_axis=0,
                    concat_axis=1,
                    tiled=True,
                )
            ),
            join_heads(
                lax.all_to_all(
                    back_rows(pixel_vgrad).astype(jnp.bfloat16),
                    "seq",
                    split_axis=0,
                    concat_axis=1,
                    tiled=True,
                )
            ),
        ]
    )
    caption_all = lax.all_gather(caption_kv, "seq", axis=0, tiled=True)
    caption_rows = caption_all.shape[0]
    caption_keys = caption_all[:, 0].reshape(1, caption_rows, head_count, HDIM)
    caption_values = caption_all[:, 1].reshape(1, caption_rows, head_count, HDIM)
    caption_keep = jnp.arange(caption_rows) < caption_len[0]
    cross_rows = split_heads(cross_query, 1)
    cross_grad = split_heads(grad_rows, 1)
    cross_results = attend_forward(
        cross_rows, caption_keys, caption_values, cross_grad, caption_keep
    )
    row_count = caption_kv.shape[0] * lax.axis_size("seq")
    slope_part = cross_results[3]
    weight_part = cross_results[2]
    key_part, value_part = key_terms(cross_rows, cross_grad, weight_part, slope_part)
    caption_grads = lax.psum_scatter(
        jnp.stack(
            [
                key_part.reshape(row_count, feature_width),
                value_part.reshape(row_count, feature_width),
            ],
            axis=1,
        ),
        "seq",
        scatter_dimension=0,
        tiled=True,
    )
    total_rows = (
        join_heads(spatial_out).astype(jnp.float32)
        + join_heads(
            lax.all_to_all(back_rows(outcome[0]), "seq", split_axis=0, concat_axis=1, tiled=True)
        ).astype(jnp.float32)
        + join_heads(cross_results[0]).astype(jnp.float32)
    )
    mixed = jnp.where(live_rows[:, None], total_rows, 0.0).astype(jnp.bfloat16)
    cross_query_grad = join_heads(cross_results[1]).astype(jnp.bfloat16)
    return (mixed, spatial_grads, temporal_grads, cross_query_grad, caption_grads)


def solution(mesh):
    placed = (
        P(None, ("dp", "seq"), None),
        P(None, ("dp", "seq"), None),
        P(("dp", "seq"), None),
        P(("dp", "seq"), None, None),
        P(("dp", "seq"), None),
        P("dp"),
        P("dp"),
    )
    return jax.shard_map(
        local,
        mesh=mesh,
        in_specs=placed,
        out_specs=(
            P(("dp", "seq"), None),
            P(None, ("dp", "seq"), None),
            P(None, ("dp", "seq"), None),
            P(("dp", "seq"), None),
            P(("dp", "seq"), None, None),
        ),
        check_vma=False,
    )
```

profile of v0, /device:TPU:1, one launch (start us, length us, event | category | flops | bytes accessed | tf_op | source)
XLA Modules:
  0.0 367.2 jit_solution(1501394457861718866)
XLA Ops:
  10.2 7.3 %all-to-all-start.4 = ((bf16[8,16,12,128]{3,0,2,1:T(8,128)(2,1)}), bf16[8,16,12,128]{3,0,2,1:T(8,128)(2,1)S(1)}, u32[]{:S(2)}, u32[]{:S(2)}) async-start(bf16[8,16,12,128]{3,0,2,1:T(8,128)(2,1)} %copy.191), calls=%async_computation.4 | async-start | bytes 786432 | tf_op jit(solution)/shard_map/all_to_all | solution.py:133
  20.2 9.3 %all-to-all-done.4 = bf16[8,16,12,128]{3,0,2,1:T(8,128)(2,1)S(1)} async-done(((bf16[8,16,12,128]{3,0,2,1:T(8,128)(2,1)}), bf16[8,16,12,128]{3,0,2,1:T(8,128)(2,1)S(1)}, u32[]{:S(2)}, u32[]{:S(2)}) %all-to-all-start.4) | async-done | bytes 393248 | tf_op jit(solution)/shard_map/all_to_all | solution.py:133
  29.5 3.8 %all-to-all-start = ((bf16[8,16,12,128]{3,0,2,1:T(8,128)(2,1)}), bf16[8,16,12,128]{3,0,2,1:T(8,128)(2,1)S(1)}, u32[]{:S(2)}, u32[]{:S(2)}) async-start(bf16[8,16,12,128]{3,0,2,1:T(8,128)(2,1)} %copy.160), calls=%async_computation | async-start | bytes 786432 | tf_op jit(solution)/shard_map/all_to_all | solution.py:124
  34.6 10.6 %all-to-all-done = bf16[8,16,12,128]{3,0,2,1:T(8,128)(2,1)S(1)} async-done(((bf16[8,16,12,128]{3,0,2,1:T(8,128)(2,1)}), bf16[8,16,12,128]{3,0,2,1:T(8,128)(2,1)S(1)}, u32[]{:S(2)}, u32[]{:S(2)}) %all-to-all-start) | async-done | bytes 393248 | tf_op jit(solution)/shard_map/all_to_all | solution.py:124
  45.2 3.8 %all-to-all-start.1 = ((bf16[8,16,12,128]{3,0,2,1:T(8,128)(2,1)}), bf16[8,16,12,128]{3,0,2,1:T(8,128)(2,1)S(1)}, u32[]{:S(2)}, u32[]{:S(2)}) async-start(bf16[8,16,12,128]{3,0,2,1:T(8,128)(2,1)} %copy.163), calls=%async_computation.1 | async-start | bytes 786432 | tf_op jit(solution)/shard_map/all_to_all | solution.py:127
  50.3 10.6 %all-to-all-done.1 = bf16[8,16,12,128]{3,0,2,1:T(8,128)(2,1)S(1)} async-done(((bf16[8,16,12,128]{3,0,2,1:T(8,128)(2,1)}), bf16[8,16,12,128]{3,0,2,1:T(8,128)(2,1)S(1)}, u32[]{:S(2)}, u32[]{:S(2)}) %all-to-all-start.1) | async-done | bytes 393248 | tf_op jit(solution)/shard_map/all_to_all | solution.py:127
  60.9 3.8 %all-to-all-start.2 = ((bf16[8,16,12,128]{3,0,2,1:T(8,128)(2,1)}), bf16[8,16,12,128]{3,0,2,1:T(8,128)(2,1)S(1)}, u32[]{:S(2)}, u32[]{:S(2)}) async-start(bf16[8,16,12,128]{3,0,2,1:T(8,128)(2,1)} %copy.166), calls=%async_computation.2 | async-start | bytes 786432 | tf_op jit(solution)/shard_map/all_to_all | solution.py:130
  65.2 2.3 fusion.70
  67.5 1.7 fusion.24
  70.1 6.5 %all-to-all-done.2 = bf16[8,16,12,128]{3,0,2,1:T(8,128)(2,1)S(1)} async-done(((bf16[8,16,12,128]{3,0,2,1:T(8,128)(2,1)}), bf16[8,16,12,128]{3,0,2,1:T(8,128)(2,1)S(1)}, u32[]{:S(2)}, u32[]{:S(2)}) %all-to-all-start.2) | async-done | bytes 393248 | tf_op jit(solution)/shard_map/all_to_all | solution.py:130
  76.6 3.8 %all-to-all-start.7 = ((bf16[128,1,12,128]{3,2,1,0:T(8,128)(2,1)}), bf16[128,1,12,128]{3,2,1,0:T(8,128)(2,1)S(1)}, u32[]{:S(2)}, u32[]{:S(2)}) async-start(bf16[128,1,12,128]{3,2,1,0:T(8,128)(2,1)} %bitcast.76), calls=%async_computation.7 | async-start | bytes 1048576 | tf_op jit(solution)/shard_map/all_to_all | solution.py:177
  80.6 2.8 fusion.37
  85.6 9.0 %all-to-all-done.7 = bf16[128,1,12,128]{3,2,1,0:T(8,128)(2,1)S(1)} async-done(((bf16[128,1,12,128]{3,2,1,0:T(8,128)(2,1)}), bf16[128,1,12,128]{3,2,1,0:T(8,128)(2,1)S(1)}, u32[]{:S(2)}, u32[]{:S(2)}) %all-to-all-start.7) | async-done | bytes 393248 | tf_op jit(solution)/shard_map/all_to_all | solution.py:177
  94.6 4.5 %all-to-all-start.5 = ((bf16[128,1,12,128]{3,2,1,0:T(8,128)(2,1)}), bf16[128,1,12,128]{3,2,1,0:T(8,128)(2,1)S(1)}, u32[]{:S(2)}, u32[]{:S(2)}) async-start(bf16[128,1,12,128]{3,2,1,0:T(8,128)(2,1)} %bitcast.66), calls=%async_computation.5 | async-start | bytes 1048576 | tf_op jit(solution)/shard_map/all_to_all | solution.py:159
  99.6 1.7 fusion.25
  102.2 11.0 %all-to-all-done.5 = bf16[128,1,12,128]{3,2,1,0:T(8,128)(2,1)S(1)} async-done(((bf16[128,1,12,128]{3,2,1,0:T(8,128)(2,1)}), bf16[128,1,12,128]{3,2,1,0:T(8,128)(2,1)S(1)}, u32[]{:S(2)}, u32[]{:S(2)}) %all-to-all-start.5) | async-done | bytes 393248 | tf_op jit(solution)/shard_map/all_to_all | solution.py:159
  113.1 4.5 %all-to-all-start.6 = ((bf16[128,1,12,128]{3,2,1,0:T(8,128)(2,1)}), bf16[128,1,12,128]{3,2,1,0:T(8,128)(2,1)}, u32[]{:S(2)}, u32[]{:S(2)}) async-start(bf16[128,1,12,128]{3,2,1,0:T(8,128)(2,1)} %bitcast.71), calls=%async_computation.6 | async-start | bytes 1048576 | tf_op jit(solution)/shard_map/all_to_all | solution.py:168
  119.7 1.9 copy.260
  121.5 10.3 %all-to-all-done.6 = bf16[128,1,12,128]{3,2,1,0:T(8,128)(2,1)} async-done(((bf16[128,1,12,128]{3,2,1,0:T(8,128)(2,1)}), bf16[128,1,12,128]{3,2,1,0:T(8,128)(2,1)}, u32[]{:S(2)}, u32[]{:S(2)}) %all-to-all-start.6) | async-done | bytes 393248 | tf_op jit(solution)/shard_map/all_to_all | solution.py:168
  131.9 4.6 %all-to-all-start.3 = ((bf16[128,1,12,128]{3,2,1,0:T(8,128)(2,1)}), bf16[128,1,12,128]{3,2,1,0:T(8,128)(2,1)}, u32[]{:S(2)}, u32[]{:S(2)}) async-start(bf16[128,1,12,128]{3,2,1,0:T(8,128)(2,1)} %bitcast.28), calls=%async_computation.3 | async-start | bytes 1048576 | tf_op jit(solution)/shard_map/all_to_all | solution.py:216
  145.2 21.3 %all-to-all-done.3 = bf16[128,1,12,128]{3,2,1,0:T(8,128)(2,1)} async-done(((bf16[128,1,12,128]{3,2,1,0:T(8,128)(2,1)}), bf16[128,1,12,128]{3,2,1,0:T(8,128)(2,1)}, u32[]{:S(2)}, u32[]{:S(2)}) %all-to-all-start.3) | async-done | bytes 393248 | tf_op jit(solution)/shard_map/all_to_all | solution.py:216
  170.3 2.7 maximum_select_fusion
  174.0 2.9 fusion.69
  176.9 2.2 fusion.18
  182.1 2.0 fusion.75
  184.1 6.6 %fusion.66 = (bf16[320,1,1536]{2,1,0:T(2,128)(2,1)}, bf16[320,1,1536]{2,1,0:T(2,128)(2,1)}) fusion(bf16[320,2,1536]{2,1,0:T(2,128)(2,1)} %all-gather.2.cloned.1.call-done), kind=kLoop, calls=%fused_computation.110 | loop fusion | bytes 3932160 | tf_op jit(solution)/shard_map/slice | solution.py:189
  190.8 4.9 %copy.176 = bf16[320,1,1536]{0,2,1:T(8,128)(2,1)} copy(bf16[320,1,1536]{2,1,0:T(2,128)(2,1)} %get-tuple-element.24) | data formatting | bytes 1966080 | tf_op jit(solution)/shard_map/slice | solution.py:189
  195.7 5.0 %copy.179 = bf16[320,1,1536]{0,2,1:T(8,128)(2,1)} copy(bf16[320,1,1536]{2,1,0:T(2,128)(2,1)} %get-tuple-element.25) | data formatting | bytes 1966080 | tf_op jit(solution)/shard_map/slice | solution.py:190
  200.7 4.1 %fusion.68 = (f32[12,128]{1,0:T(8,128)}, f32[12,128,320]{1,2,0:T(8,128)}) fusion(pred[320]{0:T(512)(128)(4,1)S(1)} %iota_compare_fusion, bf16[128,12,128]{0,2,1:T(8,128)(2,1)S(1)} %bitcast.241, bf16[320,12,128]{0,2,1:T(8,128)(2,1)} %bitcast.234), kind=kOutput, calls=%fused_computation.112 | convolution fusion | flops 127795520 | bytes 3348800 | tf_op jit(solution)/shard_map/sub | solution.py:24
  204.8 3.5 fusion.33
  210.5 1.5 multiply_convert_fusion.1
  212.0 2.2 multiply_bitcast_fusion
  214.2 3.5 copy.189
  217.7 2.9 fusion.4
  220.7 1.7 convolution_bitcast_fusion
  222.4 3.0 copy.216
  225.4 2.9 multiply_bitcast_fusion.1
  228.4 3.0 copy.214
  231.4 4.8 %pad_maximum_fusion = f32[320,2,1536]{0,2,1:T(8,128)} fusion(f32[320,1,1536]{0,2,1:T(8,128)} %bitcast.228, f32[320,1,1536]{0,2,1:T(8,128)} %bitcast.229), kind=kLoop, calls=%fused_computation.7 | loop fusion | flops 983040 | bytes 7864320 | tf_op jit(solution)/shard_map/stack | solution.py:202
  236.2 8.0 %copy.217 = f32[320,2,1536]{2,1,0:T(2,128)} copy(f32[320,2,1536]{0,2,1:T(8,128)} %pad_maximum_fusion) | data formatting | bytes 7864320 | tf_op jit(solution)/shard_map/stack | solution.py:202
  246.2 2.6 fusion.19
  248.8 11.0 %collective-permute-done.2 = bf16[2,256,1536]{1,2,0:T(8,128)(2,1)} collective-permute-done((bf16[2,256,1536]{1,2,0:T(8,128)(2,1)}, bf16[2,256,1536]{1,2,0:T(8,128)(2,1)}, u32[]{:S(2)}, u32[]{:S(2)}) %collective-permute-start.2) | collective-permute-done | bytes 1572896 | tf_op jit(solution)/shard_map/ppermute | solution.py:11
  259.7 2.0 fusion.6
  261.8 1.6 copy-done.2
  264.4 2.7 collective-permute-start.3
  270.1 3.0 fusion.36
  273.1 82.7 %all-reduce.3.cloned.1.call-done = f32[320,2,1536]{2,1,0:T(2,128)} async-done(((f32[320,2,1536]{2,1,0:T(2,128)}), f32[320,2,1536]{2,1,0:T(2,128)}) %all-reduce.3.cloned.1.call-update) | async-done | bytes 3932176
  355.8 1.7 constant_dynamic-slice_fusion
  (139 shorter events, 40.6 us)
Async XLA Ops:
  10.2 19.3 %all-to-all-start.4 = ((bf16[8,16,12,128]{3,0,2,1:T(8,128)(2,1)}), bf16[8,16,12,128]{3,0,2,1:T(8,128)(2,1)S(1)}, u32[]{:S(2)}, u32[]{:S(2)}) async-start(bf16[8,16,12,128]{3,0,2,1:T(8,128)(2,1)} %copy.191), calls=%async_computation.4 | async-start | bytes 786432 | tf_op jit(solution)/shard_map/all_to_all | solution.py:133
  29.5 15.7 %all-to-all-start = ((bf16[8,16,12,128]{3,0,2,1:T(8,128)(2,1)}), bf16[8,16,12,128]{3,0,2,1:T(8,128)(2,1)S(1)}, u32[]{:S(2)}, u32[]{:S(2)}) async-start(bf16[8,16,12,128]{3,0,2,1:T(8,128)(2,1)} %copy.160), calls=%async_computation | async-start | bytes 786432 | tf_op jit(solution)/shard_map/all_to_all | solution.py:124
  45.2 15.7 %all-to-all-start.1 = ((bf16[8,16,12,128]{3,0,2,1:T(8,128)(2,1)}), bf16[8,16,12,128]{3,0,2,1:T(8,128)(2,1)S(1)}, u32[]{:S(2)}, u32[]{:S(2)}) async-start(bf16[8,16,12,128]{3,0,2,1:T(8,128)(2,1)} %copy.163), calls=%async_computation.1 | async-start | bytes 786432 | tf_op jit(solution)/shard_map/all_to_all | solution.py:127
  60.9 15.7 %all-to-all-start.2 = ((bf16[8,16,12,128]{3,0,2,1:T(8,128)(2,1)}), bf16[8,16,12,128]{3,0,2,1:T(8,128)(2,1)S(1)}, u32[]{:S(2)}, u32[]{:S(2)}) async-start(bf16[8,16,12,128]{3,0,2,1:T(8,128)(2,1)} %copy.166), calls=%async_computation.2 | async-start | bytes 786432 | tf_op jit(solution)/shard_map/all_to_all | solution.py:130
  65.1 2.4 copy-start.25
  76.6 17.9 %all-to-all-start.7 = ((bf16[128,1,12,128]{3,2,1,0:T(8,128)(2,1)}), bf16[128,1,12,128]{3,2,1,0:T(8,128)(2,1)S(1)}, u32[]{:S(2)}, u32[]{:S(2)}) async-start(bf16[128,1,12,128]{3,2,1,0:T(8,128)(2,1)} %bitcast.76), calls=%async_computation.7 | async-start | bytes 1048576 | tf_op jit(solution)/shard_map/all_to_all | solution.py:177
  80.6 2.8 copy-start.31
  84.0 10.5 %copy-start.30 = (bf16[32,12,4,4]{2,3,1,0:T(4,128)(2,1)}, bf16[32,12,4,4]{2,3,1,0:T(4,128)(2,1)S(1)}, u32[]{:S(2)}) copy-start(bf16[32,12,4,4]{2,3,1,0:T(4,128)(2,1)S(1)} %fusion.21) | copy-start | bytes 36868
  84.7 14.3 %slice-start = ((bf16[3,128,1536]{2,1,0:T(8,128)(2,1)}), bf16[2,128,1536]{2,1,0:T(8,128)(2,1)S(1)}, s32[]{:S(2)}) async-start(bf16[3,128,1536]{2,1,0:T(8,128)(2,1)} %param.7), calls=%async_computation.10 | async-start | bytes 1572864 | tf_op jit(solution)/shard_map/slice | solution.py:91
  94.6 4.9 %copy-start.12 = (bf16[128,1,12,128]{3,2,1,0:T(8,128)(2,1)}, bf16[128,1,12,128]{3,2,1,0:T(8,128)(2,1)S(1)}, u32[]{:S(2)}) copy-start(bf16[128,1,12,128]{3,2,1,0:T(8,128)(2,1)S(1)} %all-to-all-done.7) | copy-start | bytes 1179652
  94.6 18.6 %all-to-all-start.5 = ((bf16[128,1,12,128]{3,2,1,0:T(8,128)(2,1)}), bf16[128,1,12,128]{3,2,1,0:T(8,128)(2,1)S(1)}, u32[]{:S(2)}, u32[]{:S(2)}) async-start(bf16[128,1,12,128]{3,2,1,0:T(8,128)(2,1)} %bitcast.66), calls=%async_computation.5 | async-start | bytes 1048576 | tf_op jit(solution)/shard_map/all_to_all | solution.py:159
  99.4 18.2 %collective-permute-start = (bf16[2,128,1536]{1,2,0:T(8,128)(2,1)S(1)}, bf16[2,128,1536]{1,2,0:T(8,128)(2,1)S(1)}, u32[]{:S(2)}, u32[]{:S(2)}) collective-permute-start(bf16[2,128,1536]{1,2,0:T(8,128)(2,1)S(1)} %copy.272), channel_id=1, source_target_pairs={{0,1},{1,0},{2,3},{3,2},{4,5},{5,4},{6,7},{7,6},{8,9},{9,8},{10,11... | collective-permute-start | bytes 2359304 | tf_op jit(solution)/shard_map/ppermute | solution.py:11
  113.1 4.5 %copy-start.14 = (bf16[128,1,12,128]{3,2,1,0:T(8,128)(2,1)}, bf16[128,1,12,128]{3,2,1,0:T(8,128)(2,1)S(1)}, u32[]{:S(2)}) copy-start(bf16[128,1,12,128]{3,2,1,0:T(8,128)(2,1)S(1)} %all-to-all-done.5) | copy-start | bytes 1179652
  113.1 18.7 %all-to-all-start.6 = ((bf16[128,1,12,128]{3,2,1,0:T(8,128)(2,1)}), bf16[128,1,12,128]{3,2,1,0:T(8,128)(2,1)}, u32[]{:S(2)}, u32[]{:S(2)}) async-start(bf16[128,1,12,128]{3,2,1,0:T(8,128)(2,1)} %bitcast.71), calls=%async_computation.6 | async-start | bytes 1048576 | tf_op jit(solution)/shard_map/all_to_all | solution.py:168
  118.2 20.9 %copy-start.24 = (bf16[128,1536]{1,0:T(8,128)(2,1)S(1)}, bf16[128,1536]{1,0:T(8,128)(2,1)}, u32[]{:S(2)}) copy-start(bf16[128,1536]{1,0:T(8,128)(2,1)} %param.9) | copy-start | bytes 1179652
  118.2 52.1 %collective-permute-start.1 = (bf16[2,256,1536]{1,2,0:T(8,128)(2,1)S(1)}, bf16[2,256,1536]{1,2,0:T(8,128)(2,1)}, u32[]{:S(2)}, u32[]{:S(2)}) collective-permute-start(bf16[2,256,1536]{1,2,0:T(8,128)(2,1)S(1)} %maximum_select_fusion.1), channel_id=1, source_target_pairs={{0,2},{1,3},{2,0},{3,1},{4,6},{5,7},{6,4},{7,5},{8,10},{9,11},{10,... | collective-permute-start | bytes 4718600 | tf_op jit(solution)/shard_map/ppermute | solution.py:11
  121.5 18.5 %slice-start.1 = ((bf16[3,128,1536]{2,1,0:T(8,128)(2,1)}), bf16[1,128,1536]{2,1,0:T(8,128)(2,1)S(1)}, s32[]{:S(2)}) async-start(bf16[3,128,1536]{2,1,0:T(8,128)(2,1)} %param.7), calls=%async_computation.11 | async-start | bytes 786432 | tf_op jit(solution)/shard_map/slice | solution.py:96
  131.9 9.1 %copy-start.27 = (u32[32]{0:T(128)S(1)}, u32[32]{0:T(128)}, u32[]{:S(2)}) copy-start(u32[32]{0:T(128)} %constant.84) | copy-start | bytes 388
  131.9 10.3 %copy-start.13 = (bf16[128,1,12,128]{3,2,1,0:T(8,128)(2,1)S(1)}, bf16[128,1,12,128]{3,2,1,0:T(8,128)(2,1)}, u32[]{:S(2)}) copy-start(bf16[128,1,12,128]{3,2,1,0:T(8,128)(2,1)} %copy-done.12) | copy-start | bytes 1179652
  131.9 34.7 %all-to-all-start.3 = ((bf16[128,1,12,128]{3,2,1,0:T(8,128)(2,1)}), bf16[128,1,12,128]{3,2,1,0:T(8,128)(2,1)}, u32[]{:S(2)}, u32[]{:S(2)}) async-start(bf16[128,1,12,128]{3,2,1,0:T(8,128)(2,1)} %bitcast.28), calls=%async_computation.3 | async-start | bytes 1048576 | tf_op jit(solution)/shard_map/all_to_all | solution.py:216
  136.5 47.6 %all-gather.2.cloned.1.call-start = ((), (), s32[]{:S(2)}) async-start(), calls=%async_computation.8 | async-start | bytes 2088960 | tf_op jit(solution)/shard_map/all_gather | solution.py:187
  137.2 218.6 %all-reduce.3.cloned.1.call-start = ((), (), s32[]{:S(2)}) async-start(), calls=%async_computation.9 | async-start | bytes 7864320
  140.0 2.8 copy-start.15
  173.2 3.7 %copy-start.4 = (bf16[1,512,1536]{1,2,0:T(8,128)(2,1)}, bf16[1,512,1536]{1,2,0:T(8,128)(2,1)S(1)}, u32[]{:S(2)}) copy-start(bf16[1,512,1536]{1,2,0:T(8,128)(2,1)S(1)} %get-tuple-element.22) | copy-start | bytes 4718596
  173.2 5.9 %copy-start.6 = (bf16[1,512,1536]{1,2,0:T(8,128)(2,1)}, bf16[1,512,1536]{1,2,0:T(8,128)(2,1)S(1)}, u32[]{:S(2)}) copy-start(bf16[1,512,1536]{1,2,0:T(8,128)(2,1)S(1)} %get-tuple-element.23) | copy-start | bytes 4718596
  179.1 1.2 copy-start.1
  180.8 1.3 copy-start.22
  180.8 1.3 copy-start.17
  195.7 5.0 %copy-start.16 = (bf16[128,1536]{0,1:T(8,128)(2,1)S(1)}, bf16[128,1536]{0,1:T(8,128)(2,1)}, u32[]{:S(2)}) copy-start(bf16[128,1536]{0,1:T(8,128)(2,1)} %copy.175) | copy-start | bytes 1179652
  204.8 3.5 copy-start.7
  204.8 3.6 copy-start.10
  204.8 3.6 copy-start.18
  208.4 1.3 copy-start.23
  208.4 2.1 copy-start.28
  208.4 2.1 copy-start.32
  209.2 2.7 copy-start.5
  210.5 1.5 copy-start.21
  217.7 3.0 copy-start.19
  217.7 3.0 copy-start.29
  217.7 3.0 copy-start.33
  220.7 39.1 %collective-permute-start.2 = (bf16[2,256,1536]{1,2,0:T(8,128)(2,1)}, bf16[2,256,1536]{1,2,0:T(8,128)(2,1)}, u32[]{:S(2)}, u32[]{:S(2)}) collective-permute-start(bf16[2,256,1536]{1,2,0:T(8,128)(2,1)} %fusion.4), channel_id=1, source_target_pairs={{0,2},{1,3},{2,0},{3,1},{4,6},{5,7},{6,4},{7,5},{8,10},{9,11},{10,... | collective-permute-start | bytes 4718600 | tf_op jit(solution)/shard_map/ppermute | solution.py:11
  246.2 13.5 %copy-start = (f32[1,512,12,128]{1,3,2,0:T(8,128)S(1)}, f32[1,512,12,128]{1,3,2,0:T(8,128)}, u32[]{:S(2)}) copy-start(f32[1,512,12,128]{1,3,2,0:T(8,128)} %copy.189) | copy-start | bytes 9437188
  259.7 7.4 %copy-start.9 = (bf16[12,128,320]{1,2,0:T(8,128)(2,1)S(1)}, bf16[12,128,320]{1,2,0:T(8,128)(2,1)}, u32[]{:S(2)}) copy-start(bf16[12,128,320]{1,2,0:T(8,128)(2,1)} %multiply_convert_fusion.1) | copy-start | bytes 2949124
  261.8 1.6 copy-start.2
  263.4 3.7 %copy-start.8 = (bf16[320,1,1536]{0,2,1:T(8,128)(2,1)S(1)}, bf16[320,1,1536]{0,2,1:T(8,128)(2,1)}, u32[]{:S(2)}) copy-start(bf16[320,1,1536]{0,2,1:T(8,128)(2,1)} %copy.176) | copy-start | bytes 2949124
  264.4 4.5 %copy-start.11 = (f32[128,1536]{0,1:T(8,128)S(1)}, f32[128,1536]{0,1:T(8,128)}, u32[]{:S(2)}) copy-start(f32[128,1536]{0,1:T(8,128)} %bitcast_convert_fusion) | copy-start | bytes 2359300
  264.4 93.1 %collective-permute-start.3 = (bf16[2,128,1536]{1,2,0:T(8,128)(2,1)}, bf16[2,128,1536]{1,2,0:T(8,128)(2,1)}, u32[]{:S(2)}, u32[]{:S(2)}) collective-permute-start(bf16[2,128,1536]{1,2,0:T(8,128)(2,1)} %dynamic-slice_convert_fusion), channel_id=1, source_target_pairs={{0,1},{1,0},{2,3},{3,2},{4,5},{5,4},{6,7},{7,6},{8,9},{9,8},{10,11... | collective-permute-start | bytes 2359304 | tf_op jit(solution)/shard_map/ppermute | solution.py:11
  270.1 87.4 %copy-start.3 = (f32[2,256,1536]{1,2,0:T(8,128)S(1)}, f32[2,256,1536]{1,2,0:T(8,128)}, u32[]{:S(2)}) copy-start(f32[2,256,1536]{1,2,0:T(8,128)} %copy-done.2) | copy-start | bytes 9437188
  (2 other events, 2.0 us)
Sparse Core Ops, SparseCore 0:
  139.6 43.2 all-gather.1
  244.4 111.3 all-reduce.2
where the time goes:
time: 371 us; the launch traced here: 367 us
  waiting for transfers between devices  183 us (49%)
  local copies, waits for them, and re-layouts  67.4 us (18%)
  starting transfers between devices  40.8 us (11%)
  matrix products  35.2 us (9%)
  other arithmetic  24.2 us (7%)
  between operations  16.5 us (4%)
    unnamed x3, waiting for transfers between devices  83.4 us
    all_to_all x1, waiting for transfers between devices, local(): lax.all_to_all(back_rows(outcome[0]), 'seq', split_axis=0, concat_axis=1,...  21.3 us
    unnamed x75, local copies, waits for them, and re-layouts  12.7 us
    slice x2, local copies, waits for them, and re-layouts, local(): caption_keys = caption_all[:, 0].reshape(1, caption_rows, head_count, HDIM)  11.6 us
    ppermute x4, waiting for transfers between devices, swapped(): lax.ppermute(shard, axis, [(i, i ^ 1 << apart) for i in range(lax.axis_si...  11 us
    all_to_all x1, waiting for transfers between devices, local(): lax.all_to_all(back_rows(outcome[1]).astype(jnp.bfloat16), 'seq', split_a...  11 us
    all_to_all x1, waiting for transfers between devices, local(): lax.all_to_all(pixel_split(temporal_qkv[0]), 'seq', split_axis=1, concat_...  10.6 us
    all_to_all x1, waiting for transfers between devices, local(): lax.all_to_all(pixel_split(temporal_qkv[1]), 'seq', split_axis=1, concat_...  10.6 us
  transfers between devices with their start and end apart: 14, of which 10 were waited for; matrix products, arithmetic and copies ran while one was open for 22% of the time, Pallas kernels for 0%

commit v1 on v0

v1 whole, which is shorter than its diff:
```python
import functools

import jax
import jax.numpy as jnp
from jax import lax
from jax.experimental import pallas as pl
from jax.experimental.pallas import tpu as pltpu
from jax.sharding import PartitionSpec as P

HDIM = 128
P_SIZE = 512
F32 = jnp.float32
BF16 = jnp.bfloat16
LOW = -1e30


def dot_nt(a, b):
    return lax.dot_general(a, b, (((1,), (1,)), ((), ())), preferred_element_type=F32)


def dot_tn(a, b):
    return lax.dot_general(a, b, (((0,), (0,)), ((), ())), preferred_element_type=F32)


def dot_nn(a, b):
    return lax.dot_general(a, b, (((1,), (0,)), ((), ())), preferred_element_type=F32)


def flat(x):
    rows = 1
    for n in x.shape[:-1]:
        rows *= n
    if x.shape[-2] % 16:
        return x.astype(F32).reshape(rows, x.shape[-1]).astype(BF16)
    return x.reshape(rows, x.shape[-1])


def unflat(x, shape):
    if shape[-2] % 16:
        return x.reshape(shape).astype(BF16)
    return x.astype(BF16).reshape(shape)


def slopes(q, k, v, g, scale, bias):
    s = dot_nt(k, q) * scale
    if bias is not None:
        s = s + bias
    p = jnp.exp(s - jnp.max(s, axis=0, keepdims=True))
    w = p * (1.0 / jnp.sum(p, axis=0, keepdims=True))
    dp = dot_nt(v, g)
    delta = jnp.sum(w * dp, axis=0, keepdims=True)
    return w.astype(BF16), (w * (dp - delta)).astype(BF16)


def kernel(
    geo,
    live_ref, clen_ref, sqkv, tqkv, cq, cap, og,
    mixed, sgrad, tgrad, cqgrad, capgrad,
    srecv, sres, trecv, tres, crecv, cf, ckv, cbias, cacc, cg, cgr, fin, spo, tmo, wbuf, dbuf,
    loc, t_s, t_r, tb_s, tb_r, s_s, s_r, sb_s, sb_r, c1_s, c1_r, c2_s, c2_r, c3_s, c3_r, c4_s, c4_r,
):
    G, F, pix, W, HC, R, RP = geo
    S = G * F
    KP = S * RP
    T = F * pix
    scale = HDIM ** (-0.5)
    dev = lax.axis_index("seq")
    f = dev // G
    g = dev % G
    live = live_ref[0]
    clen = clen_ref[0]

    def cols(i):
        return pl.ds(pl.multiple_of(i * W, 128), W)

    def hcols(h):
        return pl.ds(pl.multiple_of(h * HDIM, 128), HDIM)

    def mate(o):
        return (g + o) % G

    def mate_from(o):
        return (g + G - o) % G

    def line(o):
        return (f + o) % F

    def line_from(o):
        return (f + F - o) % F

    def at_mate(i):
        return f * G + i

    def at_line(i):
        return i * G + g

    def remote(src, dst, ss, rs, to):
        return pltpu.make_async_remote_copy(
            src_ref=src, dst_ref=dst, send_sem=ss, recv_sem=rs,
            device_id={"seq": to}, device_id_type=pl.DeviceIdType.MESH,
        )

    barrier = pltpu.get_barrier_semaphore()
    for o in range(1, G):
        pl.semaphore_signal(barrier, inc=1, device_id={"seq": at_mate(mate(o))}, device_id_type=pl.DeviceIdType.MESH)
    for o in range(1, F):
        pl.semaphore_signal(barrier, inc=1, device_id={"seq": at_line(line(o))}, device_id_type=pl.DeviceIdType.MESH)

    local = [
        pltpu.make_async_copy(cap.at[:, :, cols(g)], crecv.at[dev], loc.at[0]),
        pltpu.make_async_copy(sqkv.at[:, :, :, cols(g)], srecv.at[pl.ds(0, 3), g], loc.at[1]),
        pltpu.make_async_copy(og.at[:, :, cols(g)], srecv.at[3, g], loc.at[2]),
        pltpu.make_async_copy(cq.at[:, :, cols(g)], srecv.at[4, g], loc.at[3]),
    ]
    for c in range(G):
        local.append(pltpu.make_async_copy(tqkv.at[:, f, :, cols(c)], trecv.at[c, pl.ds(0, 3), f], loc.at[4 + 2 * c]))
        local.append(pltpu.make_async_copy(og.at[f, :, cols(c)], trecv.at[c, 3, f], loc.at[5 + 2 * c]))
    for copy in local:
        copy.start()
    pl.semaphore_wait(barrier, G + F - 2)

    def c1(o):
        return remote(cap.at[:, :, cols(mate(o))], crecv.at[dev], c1_s.at[o], c1_r.at[o], at_mate(mate(o)))

    def c1_in(o):
        i = mate_from(o)
        return remote(cap.at[:, :, cols(i)], crecv.at[at_mate(i)], c1_s.at[o], c1_r.at[o], at_mate(i))

    def t_out(c, o):
        j = line(o)
        return (
            remote(tqkv.at[:, j, :, cols(c)], trecv.at[c, pl.ds(0, 3), f], t_s.at[c, o, 0], t_r.at[c, o, 0], at_line(j)),
            remote(og.at[j, :, cols(c)], trecv.at[c, 3, f], t_s.at[c, o, 1], t_r.at[c, o, 1], at_line(j)),
        )

    def t_in(c, o):
        j = line_from(o)
        return (
            remote(tqkv.at[:, j, :, cols(c)], trecv.at[c, pl.ds(0, 3), j], t_s.at[c, o, 0], t_r.at[c, o, 0], at_line(j)),
            remote(og.at[j, :, cols(c)], trecv.at[c, 3, j], t_s.at[c, o, 1], t_r.at[c, o, 1], at_line(j)),
        )

    def s_out(o):
        i = mate(o)
        return (
            remote(sqkv.at[:, :, :, cols(i)], srecv.at[pl.ds(0, 3), g], s_s.at[o, 0], s_r.at[o, 0], at_mate(i)),
            remote(og.at[:, :, cols(i)], srecv.at[3, g], s_s.at[o, 1], s_r.at[o, 1], at_mate(i)),
            remote(cq.at[:, :, cols(i)], srecv.at[4, g], s_s.at[o, 2], s_r.at[o, 2], at_mate(i)),
        )

    def s_in(o):
        i = mate_from(o)
        return (
            remote(sqkv.at[:, :, :, cols(i)], srecv.at[pl.ds(0, 3), i], s_s.at[o, 0], s_r.at[o, 0], at_mate(i)),
            remote(og.at[:, :, cols(i)], srecv.at[3, i], s_s.at[o, 1], s_r.at[o, 1], at_mate(i)),
            remote(cq.at[:, :, cols(i)], srecv.at[4, i], s_s.at[o, 2], s_r.at[o, 2], at_mate(i)),
        )

    for o in range(1, G):
        c1(o).start()
    for o in range(1, F):
        for copy in t_out(0, o):
            copy.start()
    for o in range(1, G):
        for copy in s_out(o):
            copy.start()
    for c in range(1, G):
        for o in range(1, F):
            for copy in t_out(c, o):
                copy.start()

    def c2(o):
        rows = pl.ds(f * G, G)
        return remote(crecv.at[rows], crecv.at[rows], c2_s.at[o], c2_r.at[o], at_line(line(o)))

    def c2_in(o):
        rows = pl.ds(line_from(o) * G, G)
        return remote(crecv.at[rows], crecv.at[rows], c2_s.at[o], c2_r.at[o], at_line(line_from(o)))

    local[0].wait()
    for o in range(1, G):
        c1_in(o).wait_recv()
    for o in range(1, F):
        c2(o).start()

    cf[...] = jnp.zeros(cf.shape, F32)
    cbias[...] = jnp.full(cbias.shape, LOW, F32)

    def live_rows(x, first):
        ids = first + lax.broadcasted_iota(jnp.int32, x.shape, 0)
        return jnp.where(ids < live, x.astype(F32), 0.0).astype(BF16)

    def many(k, v, q, gr, keys, bias):
        for b in range(G):
            rows = slice(b * T, (b + 1) * T)
            w, d = slopes(q[rows], k, v, gr[rows], scale, bias)
            wbuf[pl.ds(0, keys), rows] = w
            dbuf[pl.ds(0, keys), rows] = d
        w = wbuf[pl.ds(0, keys), :]
        d = dbuf[pl.ds(0, keys), :]
        return dot_tn(w, v), dot_tn(d, k) * scale, dot_nn(d, q) * scale, dot_nn(w, gr)

    for copy in local[1:4]:
        copy.wait()
    for o in range(1, G):
        for copy in s_in(o):
            copy.wait_recv()

    block = (G, F, pix, HDIM)

    @pl.loop(0, HC)
    def _(h):
        at = hcols(h)
        q, k, v = (flat(srecv[i, :, :, :, at]) for i in range(3))
        gr = live_rows(flat(srecv[3, :, :, :, at]), f * (G * T))
        out, dq, dk, dv = many(k, v, q, gr, G * T, None)
        sres[0, :, :, :, at] = unflat(out, block)
        sres[1, :, :, :, at] = unflat(dq, block)
        sres[2, :, :, :, at] = unflat(dk, block)
        sres[3, :, :, :, at] = unflat(dv, block)

    def sb_grads(o, i, src_i):
        return remote(sres.at[pl.ds(1, 3), i], sgrad.at[:, :, :, cols(src_i)], sb_s.at[o, 0], sb_r.at[o, 0], at_mate(i))

    def sb_cross(o, i, src_i):
        return (
            remote(sres.at[0, i], spo.at[:, :, cols(src_i)], sb_s.at[o, 1], sb_r.at[o, 1], at_mate(i)),
            remote(sres.at[4, i], cqgrad.at[:, :, cols(src_i)], sb_s.at[o, 2], sb_r.at[o, 2], at_mate(i)),
        )

    for o in range(1, G):
        sb_grads(o, mate(o), g).start()
    home = [pltpu.make_async_copy(sres.at[pl.ds(1, 3), g], sgrad.at[:, :, :, cols(g)], loc.at[0])]
    home[0].start()

    rk = lax.broadcasted_iota(jnp.int32, (T, T), 0)
    rq = lax.broadcasted_iota(jnp.int32, (T, T), 1)
    shift = pix.bit_length() - 1
    first = g * T + f * pix
    key_token = (rk >> shift) * P_SIZE + (rk & (pix - 1)) + first
    same = ((rk & (pix - 1)) == (rq & (pix - 1))) & (key_token < live)
    tbias = jnp.where(same, 0.0, LOW)
    rd = lax.broadcasted_iota(jnp.int32, (T, HDIM), 0)
    t_live = ((rd >> shift) * P_SIZE + (rd & (pix - 1)) + first) < live

    def tb(c, o, j, src_j):
        return (
            remote(tres.at[c, 0, j], tmo.at[src_j, :, cols(c)], tb_s.at[c, o, 0], tb_r.at[c, o, 0], at_line(j)),
            remote(tres.at[c, pl.ds(1, 3), j], tgrad.at[:, src_j, :, cols(c)], tb_s.at[c, o, 1], tb_r.at[c, o, 1], at_line(j)),
        )

    tblock = (F, pix, HDIM)

    for c in range(G):
        local[4 + 2 * c].wait()
        local[5 + 2 * c].wait()

    @pl.loop(0, G)
    def _(c):
        for o in range(1, F):
            for copy in t_in(c, o):
                copy.wait_recv()
        for h in range(HC):
            at = pl.ds(h * HDIM, HDIM)
            q, k, v, gr = (flat(trecv[c, i, :, :, at]) for i in range(4))
            gr = jnp.where(t_live, gr.astype(F32), 0.0).astype(BF16)
            w, d = slopes(q, k, v, gr, scale, tbias)
            tres[c, 0, :, :, at] = unflat(dot_tn(w, v), tblock)
            tres[c, 1, :, :, at] = unflat(dot_tn(d, k) * scale, tblock)
            tres[c, 2, :, :, at] = unflat(dot_nn(d, q) * scale, tblock)
            tres[c, 3, :, :, at] = unflat(dot_nn(w, gr), tblock)
        for o in range(1, F):
            for copy in tb(c, o, line(o), f):
                copy.start()

    for c in range(G):
        home.append(pltpu.make_async_copy(tres.at[c, 0, f], tmo.at[f, :, cols(c)], loc.at[4 + 2 * c]))
        home.append(pltpu.make_async_copy(tres.at[c, pl.ds(1, 3), f], tgrad.at[:, f, :, cols(c)], loc.at[5 + 2 * c]))
    for copy in home[1:]:
        copy.start()

    for o in range(1, F):
        c2_in(o).wait_recv()

    @pl.loop(0, S)
    def _(s):
        at = pl.ds(pl.multiple_of(s * RP, 8), R)
        for i in range(2):
            cf[i, at, :] = crecv[s, i].astype(F32)
        ids = s * R + lax.broadcasted_iota(jnp.int32, (R, HDIM), 0)
        cbias[at, :] = jnp.where(ids < clen, 0.0, LOW)

    ckv[...] = cf[...].astype(BF16)

    @pl.loop(0, HC)
    def _(h):
        at = hcols(h)
        q = flat(srecv[4, :, :, :, at])
        gr = live_rows(flat(srecv[3, :, :, :, at]), f * (G * T))
        k = ckv[0, :, at]
        v = ckv[1, :, at]
        out, dq, dk, dv = many(k, v, q, gr, KP, cbias[...])
        total = flat(sres[0, :, :, :, at]).astype(F32) + out
        sres[0, :, :, :, at] = unflat(total, block)
        sres[4, :, :, :, at] = unflat(dq, block)
        cacc[0, :, at] = dk
        cacc[1, :, at] = dv

    @pl.loop(0, S)
    def _(s):
        at = pl.ds(pl.multiple_of(s * RP, 8), R)
        for i in range(2):
            cg[s, i] = cacc[i, at, :].astype(BF16)

    def c3(o):
        j = line(o)
        return remote(cg.at[pl.ds(j * G, G)], cgr.at[f], c3_s.at[o], c3_r.at[o], at_line(j))

    def c3_in(o):
        j = line_from(o)
        return remote(cg.at[pl.ds(j * G, G)], cgr.at[j], c3_s.at[o], c3_r.at[o], at_line(j))

    for o in range(1, F):
        c3(o).start()
    for o in range(1, G):
        for copy in sb_cross(o, mate(o), g):
            copy.start()
    home.append(pltpu.make_async_copy(sres.at[0, g], spo.at[:, :, cols(g)], loc.at[1]))
    home.append(pltpu.make_async_copy(sres.at[4, g], cqgrad.at[:, :, cols(g)], loc.at[2]))
    home[-2].start()
    home[-1].start()

    for o in range(1, F):
        c3_in(o).wait_recv()
    for i in range(G):
        at = pl.ds(pl.multiple_of((f * G + i) * RP, 8), R)
        for b in range(2):
            total = cacc[b, at, :]
            for o in range(1, F):
                total = total + cgr[line_from(o), i, b].astype(F32)
            fin[i, b] = total

    def c4(o, i, src_i):
        return remote(fin.at[i], capgrad.at[:, :, cols(src_i)], c4_s.at[o], c4_r.at[o], at_mate(i))

    for o in range(1, G):
        c4(o, mate(o), g).start()
    home.append(pltpu.make_async_copy(fin.at[g], capgrad.at[:, :, cols(g)], loc.at[3]))
    home[-1].start()

    for o in range(1, G):
        i = mate_from(o)
        sb_grads(o, i, i).wait_recv()
        for copy in sb_cross(o, i, i):
            copy.wait_recv()
    for copy in home:
        copy.wait()

    @pl.loop(0, G)
    def _(c):
        for o in range(1, F):
            j = line_from(o)
            for copy in tb(c, o, j, j):
                copy.wait_recv()

    shape3 = (F, pix, W)
    tok = (
        dev * T
        + lax.broadcasted_iota(jnp.int32, shape3, 0) * pix
        + lax.broadcasted_iota(jnp.int32, shape3, 1)
    )
    for c in range(G):
        at = slice(c * W, (c + 1) * W)
        total = spo[:, :, at].astype(F32) + tmo[:, :, at].astype(F32)
        mixed[:, :, at] = jnp.where(tok < live, total, 0.0).astype(BF16)

    for o in range(1, G):
        i = mate_from(o)
        c4(o, i, i).wait_recv()

    for o in range(1, G):
        c1(o).wait_send()
        for copy in s_out(o):
            copy.wait_send()
        sb_grads(o, mate(o), g).wait_send()
        for copy in sb_cross(o, mate(o), g):
            copy.wait_send()
        c4(o, mate(o), g).wait_send()
    for o in range(1, F):
        c2(o).wait_send()
        c3(o).wait_send()

    @pl.loop(0, G)
    def _(c):
        for o in range(1, F):
            for copy in t_out(c, o):
                copy.wait_send()
            for copy in tb(c, o, line(o), f):
                copy.wait_send()


def local(spatial_qkv, temporal_qkv, cross_query, caption_kv, out_grad, live_tokens, caption_len):
    devices = lax.axis_size("seq")
    rows, width = out_grad.shape
    G = P_SIZE // rows
    F = devices // G
    pix = rows // F
    W = width // G
    HC = W // HDIM
    R = caption_kv.shape[0]
    RP = (R + 7) // 8 * 8
    S = G * F
    KP = S * RP
    keys = max(KP, G * rows)
    geo = (G, F, pix, W, HC, R, RP)
    dma = pltpu.SemaphoreType.DMA
    any_spec = pl.BlockSpec(memory_space=pl.ANY)
    smem = pl.BlockSpec(memory_space=pltpu.SMEM)
    vmem = pl.BlockSpec(memory_space=pltpu.VMEM)
    mixed, sgrad, tgrad, cqgrad, capgrad = pl.pallas_call(
        functools.partial(kernel, geo),
        out_shape=(
            jax.ShapeDtypeStruct((F, pix, width), BF16),
            jax.ShapeDtypeStruct((3, F, pix, width), BF16),
            jax.ShapeDtypeStruct((3, F, pix, width), BF16),
            jax.ShapeDtypeStruct((F, pix, width), BF16),
            jax.ShapeDtypeStruct((2, R, width), F32),
        ),
        in_specs=[smem, smem] + [any_spec] * 5,
        out_specs=(vmem, any_spec, any_spec, any_spec, any_spec),
        scratch_shapes=[
            pltpu.VMEM((5, G, F, pix, W), BF16),
            pltpu.VMEM((5, G, F, pix, W), BF16),
            pltpu.VMEM((G, 4, F, pix, W), BF16),
            pltpu.VMEM((G, 4, F, pix, W), BF16),
            pltpu.VMEM((S, 2, R, W), BF16),
            pltpu.VMEM((2, KP, W), F32),
            pltpu.VMEM((2, KP, W), BF16),
            pltpu.VMEM((KP, HDIM), F32),
            pltpu.VMEM((2, KP, W), F32),
            pltpu.VMEM((S, 2, R, W), BF16),
            pltpu.VMEM((F, G, 2, R, W), BF16),
            pltpu.VMEM((G, 2, R, W), F32),
            pltpu.VMEM((F, pix, width), BF16),
            pltpu.VMEM((F, pix, width), BF16),
            pltpu.VMEM((keys, G * rows), BF16),
            pltpu.VMEM((keys, G * rows), BF16),
            dma((4 + 2 * G,)),
            dma((G, F, 2)), dma((G, F, 2)),
            dma((G, F, 2)), dma((G, F, 2)),
            dma((G, 3)), dma((G, 3)),
            dma((G, 3)), dma((G, 3)),
            dma((G,)), dma((G,)),
            dma((F,)), dma((F,)),
            dma((F,)), dma((F,)),
            dma((G,)), dma((G,)),
        ],
        compiler_params=pltpu.CompilerParams(
            collective_id=0, has_side_effects=True, vmem_limit_bytes=48 * 1024 * 1024
        ),
    )(
        live_tokens,
        caption_len,
        spatial_qkv.reshape(3, F, pix, width),
        temporal_qkv.reshape(3, F, pix, width),
        cross_query.reshape(F, pix, width),
        jnp.swapaxes(caption_kv, 0, 1),
        out_grad.reshape(F, pix, width),
    )
    return (
        mixed.reshape(rows, width),
        sgrad.reshape(3, rows, width),
        tgrad.reshape(3, rows, width),
        cqgrad.reshape(rows, width),
        jnp.swapaxes(capgrad, 0, 1),
    )


def solution(mesh):
    placed = (
        P(None, ("dp", "seq"), None),
        P(None, ("dp", "seq"), None),
        P(("dp", "seq"), None),
        P(("dp", "seq"), None, None),
        P(("dp", "seq"), None),
        P("dp"),
        P("dp"),
    )
    return jax.shard_map(
        local,
        mesh=mesh,
        in_specs=placed,
        out_specs=(
            P(("dp", "seq"), None),
            P(None, ("dp", "seq"), None),
            P(None, ("dp", "seq"), None),
            P(("dp", "seq"), None),
            P(("dp", "seq"), None, None),
        ),
        check_vma=False,
    )
```

time: 371 us -> 114 us (0.31)
  waiting for transfers between devices: 183 us -> 0 us
  Pallas kernels: 0 us -> 103 us
  local copies, waits for them, and re-layouts: 67.4 us -> 8.58 us
  starting transfers between devices: 40.8 us -> 0 us
  matrix products: 35.2 us -> 0 us
  other arithmetic: 24.2 us -> 0 us
  between operations: 16.5 us -> 1.95 us
    pallas_call x0 -> x1, Pallas kernels: none -> 103 us  [local(): pl.pallas_call(functools.partial(kernel, geo), out_shape=(jax.ShapeDtypeS...]
    all_to_all x8 -> x0, waiting for transfers between devices: 88.6 us -> none  [the longest x1 21.3 us: local(): lax.all_to_all(back_rows(outcome[0]), 'seq', split_axis=0, concat_axis=1,...]
    unnamed x3 -> x0, waiting for transfers between devices: 83.4 us -> none
    all_to_all x8 -> x0, starting transfers between devices: 36.3 us -> none  [the longest x1 7.35 us: local(): lax.all_to_all(pixel_split(grad_rows), 'seq', split_axis=1, concat_axis=0...]
    dot_general x15 -> x0, matrix products: 25.9 us -> none  [the longest x3 6.81 us: key_terms(): jnp.einsum('bhnm,bnhe->bmhe', dscores, queries, preferred_element_type=jn...]
    slice x9 -> x0, local copies, waits for them, and re-layouts: 18.1 us -> none  [the longest x2 11.6 us: local(): caption_keys = caption_all[:, 0].reshape(1, caption_rows, head_count, HDIM)]
    another operation x10 -> x0, local copies, waits for them, and re-layouts: 12.7 us -> none  [the longest x1 8.05 us: local(): jnp.stack([key_part.reshape(row_count, feature_width), value_part.reshape...]
    ppermute x4 -> x0, waiting for transfers between devices: 11 us -> none  [swapped(): lax.ppermute(shard, axis, [(i, i ^ 1 << apart) for i in range(lax.axis_si...]
  transfers between devices with their start and end apart: 14 -> 0, of which waited for: 10 -> 0; matrix products, arithmetic and copies ran while one was open for 22% -> 0% of each run, Pallas kernels for 0% -> 0%
where the time goes in v1:
time: 114 us; the launch traced here: 113 us
  Pallas kernels  103 us (90%)
  local copies, waits for them, and re-layouts  8.58 us (8%)
  between operations  1.95 us (2%)
    pallas_call x1, Pallas kernels, local(): pl.pallas_call(functools.partial(kernel, geo), out_shape=(jax.ShapeDtypeS...  103 us
    unnamed x12, local copies, waits for them, and re-layouts  8.58 us

profile of v1, /device:TPU:1, one launch (start us, length us, event | category | flops | bytes accessed | tf_op | source)
XLA Modules:
  0.0 113.1 jit_solution(4877968043682569095)
XLA Ops:
  1.9 0.9 copy.15
  2.8 0.0 copy-start
  2.9 1.3 %copy-done = bf16[3,128,1536]{2,1,0:T(8,128)(2,1)S(1)} copy-done((bf16[3,128,1536]{2,1,0:T(8,128)(2,1)S(1)}, bf16[3,128,1536]{2,1,0:T(8,128)(2,1)}, u32[]{:S(2)}) %copy-start) | copy-done | bytes 1179672
  4.1 0.0 copy-start.1
  4.1 1.0 copy-done.1
  5.1 0.0 copy-start.2
  5.1 1.0 copy-done.2
  6.1 102.6 %shard_map.110 = (bf16[4,32,1536]{2,1,0:T(8,128)(2,1)S(1)}, bf16[3,4,32,1536]{3,2,1,0:T(8,128)(2,1)S(1)}, bf16[3,4,32,1536]{3,2,1,0:T(8,128)(2,1)S(1)}, bf16[4,3...) custom-call(s32[1]{0:T(128)S(6)} %copy.20.live_ref, s32[1]{0:T(128)S(6)} %copy.21.clen_ref, ...), custom_call_target="tpu_custom_call" | custom-call | tf_op jit(solution)/shard_map/pallas_call | solution.py:420
  108.7 0.9 copy.13
  109.6 0.7 copy.22
  110.4 1.0 copy.23
  111.4 1.0 copy.24
  112.4 0.7 copy.25
Async XLA Ops:
  2.8 1.3 %copy-start = (bf16[3,128,1536]{2,1,0:T(8,128)(2,1)S(1)}, bf16[3,128,1536]{2,1,0:T(8,128)(2,1)}, u32[]{:S(2)}) copy-start(bf16[3,128,1536]{2,1,0:T(8,128)(2,1)} %param.7) | copy-start | bytes 3538948
  4.1 1.0 copy-start.1
  5.1 1.0 copy-start.2

commit v2 on v1

--- a/solution.py
+++ b/solution.py
@@ -56,7 +56,7 @@
     geo,
     live_ref, clen_ref, sqkv, tqkv, cq, cap, og,
     mixed, sgrad, tgrad, cqgrad, capgrad,
-    srecv, sres, trecv, tres, crecv, cf, ckv, cbias, cacc, cg, cgr, fin, spo, tmo, wbuf, dbuf,
+    srecv, sres, trecv, tres, crecv, cf, ckv, cbias, cacc, cg, cgu, cgd, fin, spo, tmo, wbuf, dbuf, tbias,
     loc, t_s, t_r, tb_s, tb_r, s_s, s_r, sb_s, sb_r, c1_s, c1_r, c2_s, c2_r, c3_s, c3_r, c4_s, c4_r,
 ):
     G, F, pix, W, HC, R, RP = geo
@@ -156,32 +156,51 @@
             remote(cq.at[:, :, cols(i)], srecv.at[4, i], s_s.at[o, 2], s_r.at[o, 2], at_mate(i)),
         )
 
-    for o in range(1, G):
-        c1(o).start()
-    for o in range(1, F):
-        for copy in t_out(0, o):
-            copy.start()
-    for o in range(1, G):
-        for copy in s_out(o):
-            copy.start()
-    for c in range(1, G):
+    def send_chunk(c):
         for o in range(1, F):
             for copy in t_out(c, o):
                 copy.start()
 
-    def c2(o):
-        rows = pl.ds(f * G, G)
-        return remote(crecv.at[rows], crecv.at[rows], c2_s.at[o], c2_r.at[o], at_line(line(o)))
-
-    def c2_in(o):
-        rows = pl.ds(line_from(o) * G, G)
-        return remote(crecv.at[rows], crecv.at[rows], c2_s.at[o], c2_r.at[o], at_line(line_from(o)))
+    for o in range(1, G):
+        c1(o).start()
+    send_chunk(0)
+    for o in range(1, G):
+        for copy in s_out(o):
+            copy.start()
+
+    def piece(i):
+        return pl.ds(i * G, G)
+
+    def up(i):
+        return remote(crecv.at[piece(i)], crecv.at[piece(i)], c2_s.at[0, i], c2_r.at[0, i], at_line(line(1)))
+
+    def down(i):
+        return remote(crecv.at[piece(i)], crecv.at[piece(i)], c2_s.at[1, i], c2_r.at[1, i], at_line(line_from(1)))
+
+    def gather_step(t):
+        @pl.when(f >= t)
+        def _():
+            if t > 0:
+                up(f - t).wait_recv()
+
+            @pl.when(f < F - 1)
+            def _():
+                up(f - t).start()
+
+        @pl.when(f + t < F)
+        def _():
+            if t > 0:
+                down(f + t).wait_recv()
+
+            @pl.when(f > 0)
+            def _():
+                down(f + t).start()
 
     local[0].wait()
     for o in range(1, G):
         c1_in(o).wait_recv()
-    for o in range(1, F):
-        c2(o).start()
+    gather_step(0)
+    send_chunk(1)
 
     cf[...] = jnp.zeros(cf.shape, F32)
     cbias[...] = jnp.full(cbias.shape, LOW, F32)
@@ -199,6 +218,65 @@
         w = wbuf[pl.ds(0, keys), :]
         d = dbuf[pl.ds(0, keys), :]
         return dot_tn(w, v), dot_tn(d, k) * scale, dot_nn(d, q) * scale, dot_nn(w, gr)
+
+    rk = lax.broadcasted_iota(jnp.int32, (T, T), 0)
+    rq = lax.broadcasted_iota(jnp.int32, (T, T), 1)
+    shift = pix.bit_length() - 1
+    first = g * T + f * pix
+    key_token = (rk >> shift) * P_SIZE + (rk & (pix - 1)) + first
+    same = ((rk & (pix - 1)) == (rq & (pix - 1))) & (key_token < live)
+    tbias[...] = jnp.where(same, 0.0, LOW)
+
+    def tb(c, o, j, src_j):
+        return (
+            remote(tres.at[c, 0, j], tmo.at[src_j, :, cols(c)], tb_s.at[c, o, 0], tb_r.at[c, o, 0], at_line(j)),
+            remote(tres.at[c, pl.ds(1, 3), j], tgrad.at[:, src_j, :, cols(c)], tb_s.at[c, o, 1], tb_r.at[c, o, 1], at_line(j)),
+        )
+
+    tblock = (F, pix, HDIM)
+    home = []
+
+    def temporal_chunk(c):
+        for o in range(1, F):
+            for copy in t_in(c, o):
+                copy.wait_recv()
+        rd = lax.broadcasted_iota(jnp.int32, (T, HDIM), 0)
+        t_live = ((rd >> shift) * P_SIZE + (rd & (pix - 1)) + first) < live
+        for h in range(HC):
+            at = pl.ds(h * HDIM, HDIM)
+            q, k, v, gr = (flat(trecv[c, i, :, :, at]) for i in range(4))
+            gr = jnp.where(t_live, gr.astype(F32), 0.0).astype(BF16)
+            w, d = slopes(q, k, v, gr, scale, tbias[...])
+            tres[c, 0, :, :, at] = unflat(dot_tn(w, v), tblock)
+            tres[c, 1, :, :, at] = unflat(dot_tn(d, k) * scale, tblock)
+            tres[c, 2, :, :, at] = unflat(dot_nn(d, q) * scale, tblock)
+            tres[c, 3, :, :, at] = unflat(dot_nn(w, gr), tblock)
+        for o in range(1, F):
+            for copy in tb(c, o, line(o), f):
+                copy.start()
+
+    def temporal_home(c):
+        mine = [
+            pltpu.make_async_copy(tres.at[c, 0, f], tmo.at[f, :, cols(c)], loc.at[4 + 2 * c]),
+            pltpu.make_async_copy(tres.at[c, pl.ds(1, 3), f], tgrad.at[:, f, :, cols(c)], loc.at[5 + 2 * c]),
+        ]
+        for copy in mine:
+            copy.start()
+        home.extend(mine)
+
+    for c in range(G):
+        local[4 + 2 * c].wait()
+        local[5 + 2 * c].wait()
+    for t in range(1, max(F - 1, 3)):
+        if t <= 2:
+            temporal_chunk(t - 1)
+            temporal_home(t - 1)
+        if t < F - 1:
+            gather_step(t)
+        if t + 1 < G:
+            send_chunk(t + 1)
+    for c in range(max(F - 1, 3) + 1, G):
+        send_chunk(c)
 
     for copy in local[1:4]:
         copy.wait()
@@ -230,57 +308,16 @@
 
     for o in range(1, G):
         sb_grads(o, mate(o), g).start()
-    home = [pltpu.make_async_copy(sres.at[pl.ds(1, 3), g], sgrad.at[:, :, :, cols(g)], loc.at[0])]
-    home[0].start()
-
-    rk = lax.broadcasted_iota(jnp.int32, (T, T), 0)
-    rq = lax.broadcasted_iota(jnp.int32, (T, T), 1)
-    shift = pix.bit_length() - 1
-    first = g * T + f * pix
-    key_token = (rk >> shift) * P_SIZE + (rk & (pix - 1)) + first
-    same = ((rk & (pix - 1)) == (rq & (pix - 1))) & (key_token < live)
-    tbias = jnp.where(same, 0.0, LOW)
-    rd = lax.broadcasted_iota(jnp.int32, (T, HDIM), 0)
-    t_live = ((rd >> shift) * P_SIZE + (rd & (pix - 1)) + first) < live
-
-    def tb(c, o, j, src_j):
-        return (
-            remote(tres.at[c, 0, j], tmo.at[src_j, :, cols(c)], tb_s.at[c, o, 0], tb_r.at[c, o, 0], at_line(j)),
-            remote(tres.at[c, pl.ds(1, 3), j], tgrad.at[:, src_j, :, cols(c)], tb_s.at[c, o, 1], tb_r.at[c, o, 1], at_line(j)),
-        )
-
-    tblock = (F, pix, HDIM)
-
-    for c in range(G):
-        local[4 + 2 * c].wait()
-        local[5 + 2 * c].wait()
-
-    @pl.loop(0, G)
-    def _(c):
-        for o in range(1, F):
-            for copy in t_in(c, o):
-                copy.wait_recv()
-        for h in range(HC):
-            at = pl.ds(h * HDIM, HDIM)
-            q, k, v, gr = (flat(trecv[c, i, :, :, at]) for i in range(4))
-            gr = jnp.where(t_live, gr.astype(F32), 0.0).astype(BF16)
-            w, d = slopes(q, k, v, gr, scale, tbias)
-            tres[c, 0, :, :, at] = unflat(dot_tn(w, v), tblock)
-            tres[c, 1, :, :, at] = unflat(dot_tn(d, k) * scale, tblock)
-            tres[c, 2, :, :, at] = unflat(dot_nn(d, q) * scale, tblock)
-            tres[c, 3, :, :, at] = unflat(dot_nn(w, gr), tblock)
-        for o in range(1, F):
-            for copy in tb(c, o, line(o), f):
-                copy.start()
-
-    for c in range(G):
-        home.append(pltpu.make_async_copy(tres.at[c, 0, f], tmo.at[f, :, cols(c)], loc.at[4 + 2 * c]))
-        home.append(pltpu.make_async_copy(tres.at[c, pl.ds(1, 3), f], tgrad.at[:, f, :, cols(c)], loc.at[5 + 2 * c]))
-    for copy in home[1:]:
-        copy.start()
-
-    for o in range(1, F):
-        c2_in(o).wait_recv()
+    home.append(pltpu.make_async_copy(sres.at[pl.ds(1, 3), g], sgrad.at[:, :, :, cols(g)], loc.at[0]))
+    home[-1].start()
+
+    @pl.when(f == F - 1)
+    def _():
+        up(0).wait_recv()
+
+    @pl.when(f == 0)
+    def _():
+        down(F - 1).wait_recv()
 
     @pl.loop(0, S)
     def _(s):
@@ -312,16 +349,33 @@
         for i in range(2):
             cg[s, i] = cacc[i, at, :].astype(BF16)
 
-    def c3(o):
-        j = line(o)
-        return remote(cg.at[pl.ds(j * G, G)], cgr.at[f], c3_s.at[o], c3_r.at[o], at_line(j))
-
-    def c3_in(o):
-        j = line_from(o)
-        return remote(cg.at[pl.ds(j * G, G)], cgr.at[j], c3_s.at[o], c3_r.at[o], at_line(j))
-
-    for o in range(1, F):
-        c3(o).start()
+    def c3_up(j):
+        return remote(cg.at[piece(j)], cgu.at[j], c3_s.at[0, j], c3_r.at[0, j], at_line(line(1)))
+
+    def c3_down(j):
+        return remote(cg.at[piece(j)], cgd.at[j], c3_s.at[1, j], c3_r.at[1, j], at_line(line_from(1)))
+
+    def reduce_step(t):
+        def hop(j, send, arrived):
+            if t > 0:
+                send.wait_recv()
+                cg[piece(j)] = (cg[piece(j)].astype(F32) + arrived[j].astype(F32)).astype(BF16)
+            send.start()
+
+        @pl.when(f == t)
+        def _():
+            @pl.loop(0, F - 1 - t)
+            def _(i):
+                j = F - 1 - i
+                hop(j, c3_up(j), cgu)
+
+        @pl.when(f == F - 1 - t)
+        def _():
+            @pl.loop(0, F - 1 - t)
+            def _(j):
+                hop(j, c3_down(j), cgd)
+
+    reduce_step(0)
     for o in range(1, G):
         for copy in sb_cross(o, mate(o), g):
             copy.start()
@@ -330,15 +384,27 @@
     home[-2].start()
     home[-1].start()
 
-    for o in range(1, F):
-        c3_in(o).wait_recv()
+    for t in range(1, max(F - 1, G - 1)):
+        if t + 1 < G:
+            temporal_chunk(t + 1)
+            temporal_home(t + 1)
+        if t < F - 1:
+            reduce_step(t)
+
     for i in range(G):
         at = pl.ds(pl.multiple_of((f * G + i) * RP, 8), R)
         for b in range(2):
-            total = cacc[b, at, :]
-            for o in range(1, F):
-                total = total + cgr[line_from(o), i, b].astype(F32)
-            fin[i, b] = total
+            fin[i, b] = cacc[b, at, :]
+
+    @pl.when(f > 0)
+    def _():
+        c3_up(f).wait_recv()
+        fin[...] += cgu[f].astype(F32)
+
+    @pl.when(f < F - 1)
+    def _():
+        c3_down(f).wait_recv()
+        fin[...] += cgd[f].astype(F32)
 
     def c4(o, i, src_i):
         return remote(fin.at[i], capgrad.at[:, :, cols(src_i)], c4_s.at[o], c4_r.at[o], at_mate(i))
@@ -386,9 +452,30 @@
         for copy in sb_cross(o, mate(o), g):
             copy.wait_send()
         c4(o, mate(o), g).wait_send()
-    for o in range(1, F):
-        c2(o).wait_send()
-        c3(o).wait_send()
+
+    @pl.when(f < F - 1)
+    def _():
+        @pl.loop(0, F)
+        def _(i):
+            @pl.when(i <= f)
+            def _():
+                up(i).wait_send()
+
+            @pl.when(i > f)
+            def _():
+                c3_up(i).wait_send()
+
+    @pl.when(f > 0)
+    def _():
+        @pl.loop(0, F)
+        def _(i):
+            @pl.when(i >= f)
+            def _():
+                down(i).wait_send()
+
+            @pl.when(i < f)
+            def _():
+                c3_down(i).wait_send()
 
     @pl.loop(0, G)
     def _(c):
@@ -440,23 +527,25 @@
             pltpu.VMEM((2, KP, W), F32),
             pltpu.VMEM((S, 2, R, W), BF16),
             pltpu.VMEM((F, G, 2, R, W), BF16),
+            pltpu.VMEM((F, G, 2, R, W), BF16),
             pltpu.VMEM((G, 2, R, W), F32),
             pltpu.VMEM((F, pix, width), BF16),
             pltpu.VMEM((F, pix, width), BF16),
             pltpu.VMEM((keys, G * rows), BF16),
             pltpu.VMEM((keys, G * rows), BF16),
+            pltpu.VMEM((rows, rows), F32),
             dma((4 + 2 * G,)),
             dma((G, F, 2)), dma((G, F, 2)),
             dma((G, F, 2)), dma((G, F, 2)),
             dma((G, 3)), dma((G, 3)),
             dma((G, 3)), dma((G, 3)),
             dma((G,)), dma((G,)),
-            dma((F,)), dma((F,)),
-            dma((F,)), dma((F,)),
+            dma((2, F)), dma((2, F)),
+            dma((2, F)), dma((2, F)),
             dma((G,)), dma((G,)),
         ],
         compiler_params=pltpu.CompilerParams(
-            collective_id=0, has_side_effects=True, vmem_limit_bytes=48 * 1024 * 1024
+            collective_id=0, has_side_effects=True, vmem_limit_bytes=60 * 1024 * 1024
         ),
     )(
         live_tokens,

time: 114 us -> 100 us (0.88)
  Pallas kernels: 103 us -> 89.2 us
    pallas_call x1, Pallas kernels: 103 us -> 89.2 us  [local(): pl.pallas_call(functools.partial(kernel, geo), out_shape=(jax.ShapeDtypeS...]
where the time goes in v2:
time: 100 us
  Pallas kernels  89.2 us (89%)
  local copies, waits for them, and re-layouts  8.96 us (9%)
  between operations  1.95 us (2%)
    pallas_call x1, Pallas kernels, local(): pl.pallas_call(functools.partial(kernel, geo), out_shape=(jax.ShapeDtypeS...  89.2 us
    unnamed x12, local copies, waits for them, and re-layouts  8.96 us

profile of v2, /device:TPU:1, one launch (start us, length us, event | category | flops | bytes accessed | tf_op | source)
XLA Modules:
  0.0 100.1 jit_solution(9369080204948931296)
XLA Ops:
  1.9 1.6 %copy.15 = bf16[20,2,1536]{2,0,1:T(8,128)(2,1)} copy(bf16[20,2,1536]{2,1,0:T(2,128)(2,1)} %param.10) | data formatting | bytes 245760 | tf_op args[3]
  3.5 89.2 %shard_map.110 = (bf16[4,32,1536]{2,1,0:T(8,128)(2,1)}, bf16[3,4,32,1536]{3,2,1,0:T(8,128)(2,1)}, bf16[3,4,32,1536]{3,2,1,0:T(8,128)(2,1)}, bf16[4,32,1536]{2,1,0:T(8,128)(2,1)}, f32[2,20,1536]{2,1,0:T(8,128)}) custom-call(s32[1]{0:T(128)S(6)} %copy.20.live_ref, s32[1]{0:T(128)S(6)} %copy.21.clen_ref, bf16[3,4,32,1536]{3,2,1,0:T(8,128)(2,1)} %bitcast.12, ...), custom_call_target="tpu_custom_call" | custom-call | tf_op jit(solution)/shard_map/pallas_call | solution.py:507
  92.7 0.0 copy-start.1
  92.8 1.9 %copy.13 = f32[20,2,1536]{2,1,0:T(2,128)} copy(f32[20,2,1536]{2,0,1:T(8,128)} %bitcast.21) | data formatting | bytes 491520
  94.7 1.8 %copy.22 = bf16[128,1536]{1,0:T(8,128)(2,1)} copy(bf16[128,1536]{1,0:T(8,128)(2,1)} %bitcast.20) | data formatting | bytes 786432
  96.5 0.0 copy-done.1
  96.5 0.0 copy-start
  96.5 1.0 %copy.23 = bf16[3,128,1536]{2,1,0:T(8,128)(2,1)} copy(bf16[3,128,1536]{2,1,0:T(8,128)(2,1)S(1)} %bitcast.15) | data formatting | bytes 2359296
  97.5 0.7 copy-done
  98.2 0.0 copy-start.2
  98.2 1.0 %copy.24 = bf16[3,128,1536]{2,1,0:T(8,128)(2,1)} copy(bf16[3,128,1536]{2,1,0:T(8,128)(2,1)S(1)} %bitcast.14) | data formatting | bytes 2359296
  99.2 0.2 copy-done.2
  99.4 0.7 copy.25
Async XLA Ops:
  92.7 3.7 %copy-start.1 = (bf16[3,4,32,1536]{3,2,1,0:T(8,128)(2,1)S(1)}, bf16[3,4,32,1536]{3,2,1,0:T(8,128)(2,1)}, u32[]{:S(2)}) copy-start(bf16[3,4,32,1536]{3,2,1,0:T(8,128)(2,1)} %get-tuple-element.11) | copy-start | bytes 3538948
  96.5 1.7 %copy-start = (bf16[3,4,32,1536]{3,2,1,0:T(8,128)(2,1)S(1)}, bf16[3,4,32,1536]{3,2,1,0:T(8,128)(2,1)}, u32[]{:S(2)}) copy-start(bf16[3,4,32,1536]{3,2,1,0:T(8,128)(2,1)} %get-tuple-element.12) | copy-start | bytes 3538948
  98.2 1.2 %copy-start.2 = (bf16[4,32,1536]{2,1,0:T(8,128)(2,1)S(1)}, bf16[4,32,1536]{2,1,0:T(8,128)(2,1)}, u32[]{:S(2)}) copy-start(bf16[4,32,1536]{2,1,0:T(8,128)(2,1)} %get-tuple-element.13) | copy-start | bytes 1179652

commit v3 on v2

--- a/solution.py
+++ b/solution.py
@@ -54,9 +54,9 @@
 
 def kernel(
     geo,
-    live_ref, clen_ref, sqkv, tqkv, cq, cap, og,
+    live_ref, clen_ref, sqkv, tqkv, cq, cap_in, og,
     mixed, sgrad, tgrad, cqgrad, capgrad,
-    srecv, sres, trecv, tres, crecv, cf, ckv, cbias, cacc, cg, cgu, cgd, fin, spo, tmo, wbuf, dbuf, tbias,
+    srecv, sres, trecv, tres, crecv, cf, ckv, cbias, cacc, cg, cgu, cgd, fin, spo, tmo, wbuf, dbuf, tbias, cap,
     loc, t_s, t_r, tb_s, tb_r, s_s, s_r, sb_s, sb_r, c1_s, c1_r, c2_s, c2_r, c3_s, c3_r, c4_s, c4_r,
 ):
     G, F, pix, W, HC, R, RP = geo
@@ -106,6 +106,9 @@
     for o in range(1, F):
         pl.semaphore_signal(barrier, inc=1, device_id={"seq": at_line(line(o))}, device_id_type=pl.DeviceIdType.MESH)
 
+    for i in range(2):
+        cap[i] = cap_in[:, i, :]
+
     local = [
         pltpu.make_async_copy(cap.at[:, :, cols(g)], crecv.at[dev], loc.at[0]),
         pltpu.make_async_copy(sqkv.at[:, :, :, cols(g)], srecv.at[pl.ds(0, 3), g], loc.at[1]),
@@ -163,10 +166,13 @@
 
     for o in range(1, G):
         c1(o).start()
-    send_chunk(0)
-    for o in range(1, G):
-        for copy in s_out(o):
-            copy.start()
+    for o in range(1, max(F, G)):
+        if o < F:
+            for copy in t_out(0, o):
+                copy.start()
+        if o < G:
+            for copy in s_out(o):
+                copy.start()
 
     def piece(i):
         return pl.ds(i * G, G)
@@ -311,6 +317,9 @@
     home.append(pltpu.make_async_copy(sres.at[pl.ds(1, 3), g], sgrad.at[:, :, :, cols(g)], loc.at[0]))
     home[-1].start()
 
+    temporal_chunk(2)
+    temporal_home(2)
+
     @pl.when(f == F - 1)
     def _():
         up(0).wait_recv()
@@ -384,10 +393,10 @@
     home[-2].start()
     home[-1].start()
 
-    for t in range(1, max(F - 1, G - 1)):
-        if t + 1 < G:
-            temporal_chunk(t + 1)
-            temporal_home(t + 1)
+    for t in range(1, max(F - 1, G - 2)):
+        if t + 2 < G:
+            temporal_chunk(t + 2)
+            temporal_home(t + 2)
         if t < F - 1:
             reduce_step(t)
 
@@ -484,6 +493,25 @@
                 copy.wait_send()
             for copy in tb(c, o, line(o), f):
                 copy.wait_send()
+
+
+def hand_on(*refs):
+    n = (len(refs) - 2) // 2
+    srcs, caps, dsts, capo, sem = refs[:n], refs[n], refs[n + 1 : 2 * n + 1], refs[2 * n + 1], refs[-1]
+    copies = []
+    for src, dst in zip(srcs, dsts):
+        if src.ndim == 3:
+            copies += [(src.at[i], dst.at[i]) for i in range(src.shape[0])]
+        else:
+            half = src.shape[0] // 2
+            copies += [(src.at[pl.ds(i * half, half)], dst.at[pl.ds(i * half, half)]) for i in range(2)]
+    copies = [pltpu.make_async_copy(a, b, sem.at[i]) for i, (a, b) in enumerate(copies)]
+    for copy in copies:
+        copy.start()
+    for i in range(2):
+        capo[:, i, :] = caps[i]
+    for copy in copies:
+        copy.wait()
 
 
 def local(spatial_qkv, temporal_qkv, cross_query, caption_kv, out_grad, live_tokens, caption_len):
@@ -513,7 +541,7 @@
             jax.ShapeDtypeStruct((F, pix, width), BF16),
             jax.ShapeDtypeStruct((2, R, width), F32),
         ),
-        in_specs=[smem, smem] + [any_spec] * 5,
+        in_specs=[smem, smem, any_spec, any_spec, any_spec, vmem, any_spec],
         out_specs=(vmem, any_spec, any_spec, any_spec, any_spec),
         scratch_shapes=[
             pltpu.VMEM((5, G, F, pix, W), BF16),
@@ -534,6 +562,7 @@
             pltpu.VMEM((keys, G * rows), BF16),
             pltpu.VMEM((keys, G * rows), BF16),
             pltpu.VMEM((rows, rows), F32),
+            pltpu.VMEM((2, R, width), BF16),
             dma((4 + 2 * G,)),
             dma((G, F, 2)), dma((G, F, 2)),
             dma((G, F, 2)), dma((G, F, 2)),
@@ -553,15 +582,28 @@
         spatial_qkv.reshape(3, F, pix, width),
         temporal_qkv.reshape(3, F, pix, width),
         cross_query.reshape(F, pix, width),
-        jnp.swapaxes(caption_kv, 0, 1),
+        caption_kv,
         out_grad.reshape(F, pix, width),
     )
-    return (
+    return pl.pallas_call(
+        hand_on,
+        out_shape=(
+            jax.ShapeDtypeStruct((rows, width), BF16),
+            jax.ShapeDtypeStruct((3, rows, width), BF16),
+            jax.ShapeDtypeStruct((3, rows, width), BF16),
+            jax.ShapeDtypeStruct((rows, width), BF16),
+            jax.ShapeDtypeStruct((R, 2, width), F32),
+        ),
+        in_specs=[any_spec] * 4 + [vmem],
+        out_specs=(any_spec, any_spec, any_spec, any_spec, vmem),
+        scratch_shapes=[dma((10,))],
+        compiler_params=pltpu.CompilerParams(vmem_limit_bytes=60 * 1024 * 1024),
+    )(
         mixed.reshape(rows, width),
         sgrad.reshape(3, rows, width),
         tgrad.reshape(3, rows, width),
         cqgrad.reshape(rows, width),
-        jnp.swapaxes(capgrad, 0, 1),
+        capgrad,
     )
 
 

time: 100 us -> 196 us (1.96)
  Pallas kernels: 89.2 us -> 194 us
  local copies, waits for them, and re-layouts: 8.96 us -> 0 us
    pallas_call x0 -> x1, Pallas kernels: none -> 98.1 us  [local(): pl.pallas_call(hand_on, out_shape=(jax.ShapeDtypeStruct((rows, width), BF...]
    unnamed x12 -> x0, local copies, waits for them, and re-layouts: 8.96 us -> none
    pallas_call x1, Pallas kernels: 89.2 us -> 95.6 us  [local(): pl.pallas_call(functools.partial(kernel, geo), out_shape=(jax.ShapeDtypeS...]
where the time goes in v3:
time: 196 us
  Pallas kernels  194 us (99%)
    pallas_call x1, Pallas kernels, local(): pl.pallas_call(hand_on, out_shape=(jax.ShapeDtypeStruct((rows, width), BF...  98.1 us
    pallas_call x1, Pallas kernels, local(): pl.pallas_call(functools.partial(kernel, geo), out_shape=(jax.ShapeDtypeS...  95.6 us

profile of v3, /device:TPU:1, one launch (start us, length us, event | category | flops | bytes accessed | tf_op | source)
XLA Modules:
  0.0 195.7 jit_solution(16379053740016169631)
XLA Ops:
  1.9 95.6 %shard_map.110 = (bf16[4,32,1536]{2,1,0:T(8,128)(2,1)}, bf16[3,4,32,1536]{3,2,1,0:T(8,128)(2,1)}, bf16[3,4,32,1536]{3,2,1,0:T(8,128)(2,1)}, bf16[4,32,1536]{2,1,0:T(8,128)(2,1)}, f32[2,20,1536]{2,1,0:T(8,128)}) custom-call(s32[1]{0:T(128)S(6)} %copy.12.live_ref, s32[1]{0:T(128)S(6)} %copy.13.clen_ref, bf16[3,4,32,1536]{3,2,1,0:T(8,128)(2,1)} %bitcast.8, ...), custom_call_target="tpu_custom_call" | custom-call | tf_op jit(solution)/shard_map/pallas_call | solution.py:535
  97.5 98.1 %shard_map.111 = (bf16[128,1536]{1,0:T(8,128)(2,1)}, bf16[3,128,1536]{2,1,0:T(8,128)(2,1)}, bf16[3,128,1536]{2,1,0:T(8,128)(2,1)}, bf16[128,1536]{1,0:T(8,128)(2,1)}, f32[20,2,1536]{2,1,0:T(2,128)}) custom-call(bf16[128,1536]{1,0:T(8,128)(2,1)} %bitcast.14, bf16[3,128,1536]{2,1,0:T(8,128)(2,1)} %bitcast.10, bf16[3,128,1536]{2,1,0:T(8,128)(2,1)} %bitcast.11, ...), custom_call_target="tpu_custom_call" | custom-call | tf_op jit(solution)/shard_map/pallas_call | solution.py:588

commit v4 on v3

--- a/solution.py
+++ b/solution.py
@@ -166,13 +166,10 @@
 
     for o in range(1, G):
         c1(o).start()
-    for o in range(1, max(F, G)):
-        if o < F:
-            for copy in t_out(0, o):
-                copy.start()
-        if o < G:
-            for copy in s_out(o):
-                copy.start()
+    send_chunk(0)
+    for o in range(1, G):
+        for copy in s_out(o):
+            copy.start()
 
     def piece(i):
         return pl.ds(i * G, G)
@@ -317,9 +314,6 @@
     home.append(pltpu.make_async_copy(sres.at[pl.ds(1, 3), g], sgrad.at[:, :, :, cols(g)], loc.at[0]))
     home[-1].start()
 
-    temporal_chunk(2)
-    temporal_home(2)
-
     @pl.when(f == F - 1)
     def _():
         up(0).wait_recv()
@@ -393,10 +387,10 @@
     home[-2].start()
     home[-1].start()
 
-    for t in range(1, max(F - 1, G - 2)):
-        if t + 2 < G:
-            temporal_chunk(t + 2)
-            temporal_home(t + 2)
+    for t in range(1, max(F - 1, G - 1)):
+        if t + 1 < G:
+            temporal_chunk(t + 1)
+            temporal_home(t + 1)
         if t < F - 1:
             reduce_step(t)
 
@@ -496,21 +490,26 @@
 
 
 def hand_on(*refs):
-    n = (len(refs) - 2) // 2
-    srcs, caps, dsts, capo, sem = refs[:n], refs[n], refs[n + 1 : 2 * n + 1], refs[2 * n + 1], refs[-1]
-    copies = []
-    for src, dst in zip(srcs, dsts):
+    n = 4
+    srcs, caps, dsts, capo = refs[:n], refs[n], refs[n + 1 : 2 * n + 1], refs[2 * n + 1]
+    holds, sem_in, sem_out = refs[2 * n + 2 : 3 * n + 2], refs[-2], refs[-1]
+    pieces = []
+    for src, hold, dst in zip(srcs, holds, dsts):
         if src.ndim == 3:
-            copies += [(src.at[i], dst.at[i]) for i in range(src.shape[0])]
+            pieces += [(src.at[i], hold.at[i], dst.at[i]) for i in range(src.shape[0])]
         else:
             half = src.shape[0] // 2
-            copies += [(src.at[pl.ds(i * half, half)], dst.at[pl.ds(i * half, half)]) for i in range(2)]
-    copies = [pltpu.make_async_copy(a, b, sem.at[i]) for i, (a, b) in enumerate(copies)]
-    for copy in copies:
+            pieces += [tuple(r.at[pl.ds(i * half, half)] for r in (src, hold, dst)) for i in range(2)]
+    take = [pltpu.make_async_copy(a, b, sem_in.at[i]) for i, (a, b, _) in enumerate(pieces)]
+    give = [pltpu.make_async_copy(b, c, sem_out.at[i]) for i, (_, b, c) in enumerate(pieces)]
+    for copy in take:
         copy.start()
     for i in range(2):
         capo[:, i, :] = caps[i]
-    for copy in copies:
+    for first, second in zip(take, give):
+        first.wait()
+        second.start()
+    for copy in give:
         copy.wait()
 
 
@@ -596,7 +595,14 @@
         ),
         in_specs=[any_spec] * 4 + [vmem],
         out_specs=(any_spec, any_spec, any_spec, any_spec, vmem),
-        scratch_shapes=[dma((10,))],
+        scratch_shapes=[
+            pltpu.VMEM((rows, width), BF16),
+            pltpu.VMEM((3, rows, width), BF16),
+            pltpu.VMEM((3, rows, width), BF16),
+            pltpu.VMEM((rows, width), BF16),
+            dma((10,)),
+            dma((10,)),
+        ],
         compiler_params=pltpu.CompilerParams(vmem_limit_bytes=60 * 1024 * 1024),
     )(
         mixed.reshape(rows, width),

time: 196 us -> 96.8 us (0.49)
  Pallas kernels: 194 us -> 94.7 us
    pallas_call x1, Pallas kernels: 98.1 us -> 4.54 us  [local(): pl.pallas_call(hand_on, out_shape=(jax.ShapeDtypeStruct((rows, width), BF...]
    pallas_call x1, Pallas kernels: 95.6 us -> 90.2 us  [local(): pl.pallas_call(functools.partial(kernel, geo), out_shape=(jax.ShapeDtypeS...]
where the time goes in v4:
time: 96.8 us; the launch traced here: 96.6 us
  Pallas kernels  94.7 us (98%)
  between operations  1.93 us (2%)
    pallas_call x1, Pallas kernels, local(): pl.pallas_call(functools.partial(kernel, geo), out_shape=(jax.ShapeDtypeS...  90.2 us
    pallas_call x1, Pallas kernels, local(): pl.pallas_call(hand_on, out_shape=(jax.ShapeDtypeStruct((rows, width), BF...  4.54 us

profile of v4, /device:TPU:1, one launch (start us, length us, event | category | flops | bytes accessed | tf_op | source)
XLA Modules:
  0.0 96.6 jit_solution(3603540519124967569)
XLA Ops:
  1.9 90.2 %shard_map.110 = (bf16[4,32,1536]{2,1,0:T(8,128)(2,1)}, bf16[3,4,32,1536]{3,2,1,0:T(8,128)(2,1)}, bf16[3,4,32,1536]{3,2,1,0:T(8,128)(2,1)}, bf16[4,32,1536]{2,1,0:T(8,128)(2,1)}, f32[2,20,1536]{2,1,0:T(8,128)}) custom-call(s32[1]{0:T(128)S(6)} %copy.12.live_ref, s32[1]{0:T(128)S(6)} %copy.13.clen_ref, bf16[3,4,32,1536]{3,2,1,0:T(8,128)(2,1)} %bitcast.8, ...), custom_call_target="tpu_custom_call" | custom-call | tf_op jit(solution)/shard_map/pallas_call | solution.py:534
  92.1 4.5 %shard_map.111 = (bf16[128,1536]{1,0:T(8,128)(2,1)}, bf16[3,128,1536]{2,1,0:T(8,128)(2,1)}, bf16[3,128,1536]{2,1,0:T(8,128)(2,1)}, bf16[128,1536]{1,0:T(8,128)(2,1)}, f32[20,2,1536]{2,1,0:T(2,128)}) custom-call(bf16[128,1536]{1,0:T(8,128)(2,1)} %bitcast.14, bf16[3,128,1536]{2,1,0:T(8,128)(2,1)} %bitcast.10, bf16[3,128,1536]{2,1,0:T(8,128)(2,1)} %bitcast.11, ...), custom_call_target="tpu_custom_call" | custom-call | tf_op jit(solution)/shard_map/pallas_call | solution.py:587

commit v5 on v4

--- a/solution.py
+++ b/solution.py
@@ -56,7 +56,7 @@
     geo,
     live_ref, clen_ref, sqkv, tqkv, cq, cap_in, og,
     mixed, sgrad, tgrad, cqgrad, capgrad,
-    srecv, sres, trecv, tres, crecv, cf, ckv, cbias, cacc, cg, cgu, cgd, fin, spo, tmo, wbuf, dbuf, tbias, cap,
+    srecv, sres, trecv, tres, crecv, cf, ckv, cbias, cacc, cg, cgu, cgd, fin, spo, tmo, wbuf, dbuf, tbias, cap, cap_rows, mix,
     loc, t_s, t_r, tb_s, tb_r, s_s, s_r, sb_s, sb_r, c1_s, c1_r, c2_s, c2_r, c3_s, c3_r, c4_s, c4_r,
 ):
     G, F, pix, W, HC, R, RP = geo
@@ -100,14 +100,13 @@
             device_id={"seq": to}, device_id_type=pl.DeviceIdType.MESH,
         )
 
+    cap_copy = pltpu.make_async_copy(cap_in, cap_rows, loc.at[0])
+    cap_copy.start()
     barrier = pltpu.get_barrier_semaphore()
     for o in range(1, G):
         pl.semaphore_signal(barrier, inc=1, device_id={"seq": at_mate(mate(o))}, device_id_type=pl.DeviceIdType.MESH)
     for o in range(1, F):
         pl.semaphore_signal(barrier, inc=1, device_id={"seq": at_line(line(o))}, device_id_type=pl.DeviceIdType.MESH)
-
-    for i in range(2):
-        cap[i] = cap_in[:, i, :]
 
     local = [
         pltpu.make_async_copy(cap.at[:, :, cols(g)], crecv.at[dev], loc.at[0]),
@@ -118,8 +117,9 @@
     for c in range(G):
         local.append(pltpu.make_async_copy(tqkv.at[:, f, :, cols(c)], trecv.at[c, pl.ds(0, 3), f], loc.at[4 + 2 * c]))
         local.append(pltpu.make_async_copy(og.at[f, :, cols(c)], trecv.at[c, 3, f], loc.at[5 + 2 * c]))
-    for copy in local:
-        copy.start()
+    cap_copy.wait()
+    for i in range(2):
+        cap[i] = cap_rows[:, i, :]
     pl.semaphore_wait(barrier, G + F - 2)
 
     def c1(o):
@@ -199,10 +199,14 @@
             def _():
                 down(f + t).start()
 
+    for copy in local:
+        copy.start()
     local[0].wait()
     for o in range(1, G):
         c1_in(o).wait_recv()
     gather_step(0)
+    if F > 2:
+        gather_step(1)
     send_chunk(1)
 
     cf[...] = jnp.zeros(cf.shape, F32)
@@ -274,8 +278,8 @@
         if t <= 2:
             temporal_chunk(t - 1)
             temporal_home(t - 1)
-        if t < F - 1:
-            gather_step(t)
+        if t + 1 < F - 1:
+            gather_step(t + 1)
         if t + 1 < G:
             send_chunk(t + 1)
     for c in range(max(F - 1, 3) + 1, G):
@@ -432,6 +436,7 @@
             for copy in tb(c, o, j, j):
                 copy.wait_recv()
 
+    mixed_out = []
     shape3 = (F, pix, W)
     tok = (
         dev * T
@@ -441,11 +446,17 @@
     for c in range(G):
         at = slice(c * W, (c + 1) * W)
         total = spo[:, :, at].astype(F32) + tmo[:, :, at].astype(F32)
-        mixed[:, :, at] = jnp.where(tok < live, total, 0.0).astype(BF16)
+        mix[:, :, at] = jnp.where(tok < live, total, 0.0).astype(BF16)
+        out = pltpu.make_async_copy(mix.at[:, :, pl.ds(c * W, W)], mixed.at[:, :, pl.ds(c * W, W)], loc.at[4 + 2 * c])
+        out.start()
+        mixed_out.append(out)
 
     for o in range(1, G):
         i = mate_from(o)
         c4(o, i, i).wait_recv()
+
+    for copy in mixed_out:
+        copy.wait()
 
     for o in range(1, G):
         c1(o).wait_send()
@@ -492,7 +503,7 @@
 def hand_on(*refs):
     n = 4
     srcs, caps, dsts, capo = refs[:n], refs[n], refs[n + 1 : 2 * n + 1], refs[2 * n + 1]
-    holds, sem_in, sem_out = refs[2 * n + 2 : 3 * n + 2], refs[-2], refs[-1]
+    holds, (cap_in, cap_out, sem_in, sem_out) = refs[2 * n + 2 : 3 * n + 2], refs[3 * n + 2 :]
     pieces = []
     for src, hold, dst in zip(srcs, holds, dsts):
         if src.ndim == 3:
@@ -502,13 +513,18 @@
             pieces += [tuple(r.at[pl.ds(i * half, half)] for r in (src, hold, dst)) for i in range(2)]
     take = [pltpu.make_async_copy(a, b, sem_in.at[i]) for i, (a, b, _) in enumerate(pieces)]
     give = [pltpu.make_async_copy(b, c, sem_out.at[i]) for i, (_, b, c) in enumerate(pieces)]
+    cap_take = pltpu.make_async_copy(caps, cap_in, sem_in.at[10])
+    cap_take.start()
     for copy in take:
         copy.start()
-    for i in range(2):
-        capo[:, i, :] = caps[i]
     for first, second in zip(take, give):
         first.wait()
         second.start()
+    cap_take.wait()
+    for i in range(2):
+        cap_out[:, i, :] = cap_in[i]
+    give.append(pltpu.make_async_copy(cap_out, capo, sem_out.at[10]))
+    give[-1].start()
     for copy in give:
         copy.wait()
 
@@ -530,7 +546,6 @@
     dma = pltpu.SemaphoreType.DMA
     any_spec = pl.BlockSpec(memory_space=pl.ANY)
     smem = pl.BlockSpec(memory_space=pltpu.SMEM)
-    vmem = pl.BlockSpec(memory_space=pltpu.VMEM)
     mixed, sgrad, tgrad, cqgrad, capgrad = pl.pallas_call(
         functools.partial(kernel, geo),
         out_shape=(
@@ -540,8 +555,8 @@
             jax.ShapeDtypeStruct((F, pix, width), BF16),
             jax.ShapeDtypeStruct((2, R, width), F32),
         ),
-        in_specs=[smem, smem, any_spec, any_spec, any_spec, vmem, any_spec],
-        out_specs=(vmem, any_spec, any_spec, any_spec, any_spec),
+        in_specs=[smem, smem] + [any_spec] * 5,
+        out_specs=(any_spec,) * 5,
         scratch_shapes=[
             pltpu.VMEM((5, G, F, pix, W), BF16),
             pltpu.VMEM((5, G, F, pix, W), BF16),
@@ -562,6 +577,8 @@
             pltpu.VMEM((keys, G * rows), BF16),
             pltpu.VMEM((rows, rows), F32),
             pltpu.VMEM((2, R, width), BF16),
+            pltpu.VMEM((R, 2, width), BF16),
+            pltpu.VMEM((F, pix, width), BF16),
             dma((4 + 2 * G,)),
             dma((G, F, 2)), dma((G, F, 2)),
             dma((G, F, 2)), dma((G, F, 2)),
@@ -593,15 +610,17 @@
             jax.ShapeDtypeStruct((rows, width), BF16),
             jax.ShapeDtypeStruct((R, 2, width), F32),
         ),
-        in_specs=[any_spec] * 4 + [vmem],
-        out_specs=(any_spec, any_spec, any_spec, any_spec, vmem),
+        in_specs=[any_spec] * 5,
+        out_specs=(any_spec,) * 5,
         scratch_shapes=[
             pltpu.VMEM((rows, width), BF16),
             pltpu.VMEM((3, rows, width), BF16),
             pltpu.VMEM((3, rows, width), BF16),
             pltpu.VMEM((rows, width), BF16),
-            dma((10,)),
-            dma((10,)),
+            pltpu.VMEM((2, R, width), F32),
+            pltpu.VMEM((R, 2, width), F32),
+            dma((11,)),
+            dma((11,)),
         ],
         compiler_params=pltpu.CompilerParams(vmem_limit_bytes=60 * 1024 * 1024),
     )(

time: 96.8 us -> 98.6 us (1.019)
  Pallas kernels: 94.7 us -> 96.5 us
    pallas_call x1, Pallas kernels: 90.2 us -> 93.4 us  [local(): pl.pallas_call(functools.partial(kernel, geo), out_shape=(jax.ShapeDtypeS...]
    pallas_call x1, Pallas kernels: 4.54 us -> 3.07 us  [local(): pl.pallas_call(hand_on, out_shape=(jax.ShapeDtypeStruct((rows, width), BF...]
where the time goes in v5:
time: 98.6 us; the launch traced here: 98.4 us
  Pallas kernels  96.5 us (98%)
  between operations  1.93 us (2%)
    pallas_call x1, Pallas kernels, local(): pl.pallas_call(functools.partial(kernel, geo), out_shape=(jax.ShapeDtypeS...  93.4 us
    pallas_call x1, Pallas kernels, local(): pl.pallas_call(hand_on, out_shape=(jax.ShapeDtypeStruct((rows, width), BF...  3.07 us

profile of v5, /device:TPU:1, one launch (start us, length us, event | category | flops | bytes accessed | tf_op | source)
XLA Modules:
  0.0 98.4 jit_solution(8069949361160714733)
XLA Ops:
  1.9 93.4 %shard_map.110 = (bf16[4,32,1536]{2,1,0:T(8,128)(2,1)}, bf16[3,4,32,1536]{3,2,1,0:T(8,128)(2,1)}, bf16[3,4,32,1536]{3,2,1,0:T(8,128)(2,1)}, bf16[4,32,1536]{2,1,0:T(8,128)(2,1)}, f32[2,20,1536]{2,1,0:T(8,128)}) custom-call(s32[1]{0:T(128)S(6)} %copy.12.live_ref, s32[1]{0:T(128)S(6)} %copy.13.clen_ref, bf16[3,4,32,1536]{3,2,1,0:T(8,128)(2,1)} %bitcast.8, ...), custom_call_target="tpu_custom_call" | custom-call | tf_op jit(solution)/shard_map/pallas_call | solution.py:549
  95.4 3.1 %shard_map.111 = (bf16[128,1536]{1,0:T(8,128)(2,1)}, bf16[3,128,1536]{2,1,0:T(8,128)(2,1)}, bf16[3,128,1536]{2,1,0:T(8,128)(2,1)}, bf16[128,1536]{1,0:T(8,128)(2,1)}, f32[20,2,1536]{2,1,0:T(2,128)}) custom-call(bf16[128,1536]{1,0:T(8,128)(2,1)} %bitcast.14, bf16[3,128,1536]{2,1,0:T(8,128)(2,1)} %bitcast.10, bf16[3,128,1536]{2,1,0:T(8,128)(2,1)} %bitcast.11, ...), custom_call_target="tpu_custom_call" | custom-call | tf_op jit(solution)/shard_map/pallas_call | solution.py:604

commit v6 on v5

--- a/solution.py
+++ b/solution.py
@@ -205,8 +205,6 @@
     for o in range(1, G):
         c1_in(o).wait_recv()
     gather_step(0)
-    if F > 2:
-        gather_step(1)
     send_chunk(1)
 
     cf[...] = jnp.zeros(cf.shape, F32)
@@ -278,8 +276,8 @@
         if t <= 2:
             temporal_chunk(t - 1)
             temporal_home(t - 1)
-        if t + 1 < F - 1:
-            gather_step(t + 1)
+        if t < F - 1:
+            gather_step(t)
         if t + 1 < G:
             send_chunk(t + 1)
     for c in range(max(F - 1, 3) + 1, G):

time: 98.6 us -> 94.2 us (0.955)
  Pallas kernels: 96.5 us -> 91.7 us
    pallas_call x1, Pallas kernels: 93.4 us -> 88.6 us  [local(): pl.pallas_call(functools.partial(kernel, geo), out_shape=(jax.ShapeDtypeS...]
where the time goes in v6:
time: 94.2 us; the launch traced here: 93.6 us
  Pallas kernels  91.7 us (97%)
  between operations  1.93 us (2%)
    pallas_call x1, Pallas kernels, local(): pl.pallas_call(functools.partial(kernel, geo), out_shape=(jax.ShapeDtypeS...  88.6 us
    pallas_call x1, Pallas kernels, local(): pl.pallas_call(hand_on, out_shape=(jax.ShapeDtypeStruct((rows, width), BF...  3.07 us

profile of v6, /device:TPU:1, one launch (start us, length us, event | category | flops | bytes accessed | tf_op | source)
XLA Modules:
  0.0 93.6 jit_solution(5285203321178743169)
XLA Ops:
  1.9 88.6 %shard_map.110 = (bf16[4,32,1536]{2,1,0:T(8,128)(2,1)}, bf16[3,4,32,1536]{3,2,1,0:T(8,128)(2,1)}, bf16[3,4,32,1536]{3,2,1,0:T(8,128)(2,1)}, bf16[4,32,1536]{2,1,0:T(8,128)(2,1)}, f32[2,20,1536]{2,1,0:T(8,128)}) custom-call(s32[1]{0:T(128)S(6)} %copy.12.live_ref, s32[1]{0:T(128)S(6)} %copy.13.clen_ref, bf16[3,4,32,1536]{3,2,1,0:T(8,128)(2,1)} %bitcast.8, ...), custom_call_target="tpu_custom_call" | custom-call | tf_op jit(solution)/shard_map/pallas_call | solution.py:547
  90.5 3.1 %shard_map.111 = (bf16[128,1536]{1,0:T(8,128)(2,1)}, bf16[3,128,1536]{2,1,0:T(8,128)(2,1)}, bf16[3,128,1536]{2,1,0:T(8,128)(2,1)}, bf16[128,1536]{1,0:T(8,128)(2,1)}, f32[20,2,1536]{2,1,0:T(2,128)}) custom-call(bf16[128,1536]{1,0:T(8,128)(2,1)} %bitcast.14, bf16[3,128,1536]{2,1,0:T(8,128)(2,1)} %bitcast.10, bf16[3,128,1536]{2,1,0:T(8,128)(2,1)} %bitcast.11, ...), custom_call_target="tpu_custom_call" | custom-call | tf_op jit(solution)/shard_map/pallas_call | solution.py:602

commit v7 on v6

--- a/solution.py
+++ b/solution.py
@@ -199,13 +199,13 @@
             def _():
                 down(f + t).start()
 
+    send_chunk(1)
     for copy in local:
         copy.start()
     local[0].wait()
     for o in range(1, G):
         c1_in(o).wait_recv()
     gather_step(0)
-    send_chunk(1)
 
     cf[...] = jnp.zeros(cf.shape, F32)
     cbias[...] = jnp.full(cbias.shape, LOW, F32)

time: 94.2 us -> 97 us (1.030)
  Pallas kernels: 91.7 us -> 94.9 us
    pallas_call x1, Pallas kernels: 88.6 us -> 91.8 us  [local(): pl.pallas_call(functools.partial(kernel, geo), out_shape=(jax.ShapeDtypeS...]
where the time goes in v7:
time: 97 us; the launch traced here: 96.8 us
  Pallas kernels  94.9 us (98%)
  between operations  1.93 us (2%)
    pallas_call x1, Pallas kernels, local(): pl.pallas_call(functools.partial(kernel, geo), out_shape=(jax.ShapeDtypeS...  91.8 us
    pallas_call x1, Pallas kernels, local(): pl.pallas_call(hand_on, out_shape=(jax.ShapeDtypeStruct((rows, width), BF...  3.07 us

profile of v7, /device:TPU:1, one launch (start us, length us, event | category | flops | bytes accessed | tf_op | source)
XLA Modules:
  0.0 96.8 jit_solution(5957940751128336712)
XLA Ops:
  1.9 91.8 %shard_map.110 = (bf16[4,32,1536]{2,1,0:T(8,128)(2,1)}, bf16[3,4,32,1536]{3,2,1,0:T(8,128)(2,1)}, bf16[3,4,32,1536]{3,2,1,0:T(8,128)(2,1)}, bf16[4,32,1536]{2,1,0:T(8,128)(2,1)}, f32[2,20,1536]{2,1,0:T(8,128)}) custom-call(s32[1]{0:T(128)S(6)} %copy.12.live_ref, s32[1]{0:T(128)S(6)} %copy.13.clen_ref, bf16[3,4,32,1536]{3,2,1,0:T(8,128)(2,1)} %bitcast.8, ...), custom_call_target="tpu_custom_call" | custom-call | tf_op jit(solution)/shard_map/pallas_call | solution.py:547
  93.8 3.1 %shard_map.111 = (bf16[128,1536]{1,0:T(8,128)(2,1)}, bf16[3,128,1536]{2,1,0:T(8,128)(2,1)}, bf16[3,128,1536]{2,1,0:T(8,128)(2,1)}, bf16[128,1536]{1,0:T(8,128)(2,1)}, f32[20,2,1536]{2,1,0:T(2,128)}) custom-call(bf16[128,1536]{1,0:T(8,128)(2,1)} %bitcast.14, bf16[3,128,1536]{2,1,0:T(8,128)(2,1)} %bitcast.10, bf16[3,128,1536]{2,1,0:T(8,128)(2,1)} %bitcast.11, ...), custom_call_target="tpu_custom_call" | custom-call | tf_op jit(solution)/shard_map/pallas_call | solution.py:602
